TPU v7x, 128 devices: a whole 4x4x4 slice. The times are simulated.
128 devices in a mesh: gx: 16 (over x, y), gy: 8 (over z, core).
Axes of the slice: x: 4, y: 4, z: 4, core: 2. Of those that a mesh axis runs over, the one named last changes fastest.
Arguments:
- density: bfloat16 [32768, 256], P(('gx', 'gy')), may hold values from -0.015625 to 0.015625
- pair_tiles: int32 [32768, 4], P(('gx', 'gy')), may hold values from 0 to 127, all different within a row; in each aligned block of 256 rows (0 to 255, 256 to 511, ...) at most 16 rows name the same one
- pair_slots: int32 [32768, 4, 2], P(('gx', 'gy')), may hold values from 0 to 71
- pair_sizes: int32 [32768, 2], P(('gx', 'gy')), may hold values from 4 to 16
- basis_table: bfloat16 [128, 1152, 2048], P(('gx', 'gy')), may hold values from -6 to 6
- tile_extent: int32 [128, 2, 72], P(('gx', 'gy')), may hold values from 0 to 32, as said below
Outputs:
- hamiltonian: float32 [32768, 256], P(('gx', 'gy'))
- potential: float32 [512, 512], P('gx', 'gy')
Inputs may be any that keep to these rules, and one draw needn't show every extreme that they name: `pair_tiles`: each pair names 4 different tiles; among the pairs of one device no tile is named more than 16 times, a bound that some block reaches. `pair_slots`: the same slot pair may reach one tile from several pairs; their blocks then add. `tile_extent`: the first row is below 16 and the last bound above it.
All inputs are finite; a program needn't handle non-finite values.
Results may differ from a plain program's by a relative error of at most 0.0031.
Values may be sent and summed in bfloat16 or wider, within the bound.
A program may use at most 128 MiB of HBM per device.

v0:
```python
import jax
import jax.numpy as jnp
from jax import lax
from jax.sharding import PartitionSpec as P

NB = 16
CX = 32
CY = 64


gradient_weight = 1.0


def extended(block, sides, width):
    for axis, dim in sides:
        count = lax.axis_size(axis)
        forward = [(i, i + 1) for i in range(count - 1)]
        forward.append((count - 1, 0))
        backward = [(target, source) for source, target in forward]
        low = lax.ppermute(
            lax.slice_in_dim(block, block.shape[dim] - width, None, axis=dim), axis, forward
        )
        high = lax.ppermute(lax.slice_in_dim(block, 0, width, axis=dim), axis, backward)
        block = jnp.concatenate([low, block, high], axis=dim)
    return block


def masked_basis(tables, extent, atom_slots, width):
    cell_count = tables.shape[-1]
    cell_row = lax.broadcasted_iota(jnp.int32, (atom_slots, 1, cell_count), 2) // CY
    inside = (cell_row >= extent[0][:, None, None]) & (cell_row < extent[1][:, None, None])
    shaped = tables.reshape(atom_slots, width, cell_count)
    return jnp.where(inside, shaped, jnp.zeros((), shaped.dtype))


def shards(density, pair_tiles, pair_slots, pair_sizes, basis_table, tile_extent):
    tiles_first = lax.axis_size("gx")
    tiles_second = lax.axis_size("gy")
    devices = tiles_first * tiles_second
    pair_dev, targets = pair_tiles.shape
    atom_slots = tile_extent.shape[2]
    width = NB
    capacity = max(2, 2 * pair_dev * targets // devices)
    row_index = lax.broadcasted_iota(jnp.int32, (1, width, width), 1)
    col_index = lax.broadcasted_iota(jnp.int32, (1, width, width), 2)
    size_mask = (row_index < pair_sizes[:, 0, None, None]) & (
        col_index < pair_sizes[:, 1, None, None]
    )
    size_mask = size_mask.reshape(pair_dev, width * width)
    blocks = jnp.where(size_mask, density, jnp.zeros((), density.dtype))
    first_slot = pair_slots[:, :, 0]
    second_slot = pair_slots[:, :, 1]
    factor = jnp.where(first_slot == second_slot, 1.0, 2.0).astype(jnp.bfloat16)
    outgoing = (blocks[:, None, :] * factor[:, :, None]).reshape(pair_dev * targets, width * width)
    slot_codes = (first_slot * atom_slots + second_slot).reshape(-1)
    flat_tiles = pair_tiles.reshape(-1)
    onehot = (flat_tiles[:, None] == lax.broadcasted_iota(jnp.int32, (1, devices), 1)).astype(
        jnp.int32
    )
    before = jnp.cumsum(onehot, axis=0) - onehot
    order_rank = jnp.sum(before * onehot, axis=1)
    position = flat_tiles * capacity + order_rank
    send_blocks = (
        jnp.zeros((devices * capacity, width * width), jnp.bfloat16).at[position].set(outgoing)
    )
    send_codes = jnp.zeros((devices * capacity,), jnp.int32).at[position].set(slot_codes)
    got_blocks, got_codes = (
        lax.all_to_all(send_blocks, ("gx", "gy"), split_axis=0, concat_axis=0, tiled=True),
        lax.all_to_all(send_codes, ("gx", "gy"), split_axis=0, concat_axis=0, tiled=True),
    )
    basis_three = masked_basis(basis_table[0], tile_extent[0], atom_slots, width)
    cell_count = basis_three.shape[-1]
    basis = basis_three.reshape(atom_slots * width, cell_count)
    code_table = (
        got_codes[:, None] == lax.broadcasted_iota(jnp.int32, (1, atom_slots * atom_slots), 1)
    ).astype(jnp.bfloat16)
    gathered = lax.dot_general(
        code_table, got_blocks, (((0,), (0,)), ((), ())), preferred_element_type=jnp.float32
    )
    matrix = gathered.astype(jnp.bfloat16).reshape(atom_slots, atom_slots, width, width)
    spread = jnp.einsum("abij,bjg->aig", matrix, basis_three, preferred_element_type=jnp.float32)
    charge = jnp.sum(basis * spread.reshape(atom_slots * width, cell_count), axis=0)
    charge_field = charge.reshape(CX, CY)
    padded = extended(charge_field, (("gx", 0), ("gy", 1)), 1)
    slope_first = 0.5 * (padded[2:, 1:-1] - padded[:-2, 1:-1])
    slope_second = 0.5 * (padded[1:-1, 2:] - padded[1:-1, :-2])
    potential = charge_field * lax.rsqrt(
        1.0
        + charge_field * charge_field
        + gradient_weight * (slope_first * slope_first + slope_second * slope_second)
    )
    weighted = (basis_three * potential.reshape(1, 1, cell_count)).astype(jnp.bfloat16)
    hamilton = jnp.einsum(
        "aig,bjg->abij", basis_three, weighted, preferred_element_type=jnp.float32
    ) * (CX * CY) ** (-0.5)
    flat_blocks = hamilton.reshape(atom_slots * atom_slots, width * width)
    partial_blocks = jnp.take(flat_blocks, got_codes, axis=0)
    returned = lax.all_to_all(partial_blocks, ("gx", "gy"), split_axis=0, concat_axis=0, tiled=True)
    summed = jnp.sum(returned[position].reshape(pair_dev, targets, width * width), axis=1)
    hamiltonian = jnp.where(size_mask, summed, jnp.zeros((), summed.dtype))
    return (hamiltonian, potential)


def solution(mesh):
    in_specs = (
        P(("gx", "gy"), None),
        P(("gx", "gy"), None),
        P(("gx", "gy"), None, None),
        P(("gx", "gy"), None),
        P(("gx", "gy"), None, None),
        P(("gx", "gy"), None, None),
    )
    out_specs = (P(("gx", "gy"), None), P("gx", "gy"))
    return jax.shard_map(shards, mesh=mesh, in_specs=in_specs, out_specs=out_specs, check_vma=False)
```

profile of v0, /device:TPU:1, one launch (start us, length us, event | category | flops | bytes accessed | tf_op | source)
XLA Modules:
  0.0 221.2 jit_solution(2464452803106003416)
XLA Ops:
  1.4 0.8 copy.26
  4.7 4.3 %scatter_custom_fusion = s32[2048]{0:T(1024)S(1)} fusion(s32[1024]{0:T(1024)S(1)} %bitcast.92, s32[1024]{0:T(1024)S(1)} %reshape.249, s32[]{:T(128)} %constant.24.clone.1), kind=kCustom, calls=%fused_computation.72 | custom fusion | bytes 8196 | tf_op jit(solution)/shard_map/scatter | solution.py:66
  9.7 11.5 %all-to-all-start = ((s32[128,16,1]{1,2,0:T(1,128)}), s32[128,16,1]{1,2,0:T(1,128)S(1)}, u32[]{:S(2)}, u32[]{:S(2)}) async-start(s32[128,16,1]{1,2,0:T(1,128)} %bitcast.7), calls=%async_computation | async-start | bytes 131072 | tf_op jit(solution)/shard_map/all_to_all | solution.py:69
  23.9 6.6 %scatter_custom_fusion.1 = bf16[2048,256]{1,0:T(8,128)(2,1)} fusion(s32[1024]{0:T(1024)S(1)} %bitcast.93, bf16[1024,256]{1,0:T(8,128)(2,1)S(1)} %mul.93, bf16[]{:T(256)} %constant.55.clone.1, bf16[1024]{0:T(1024)(128)(2,1)S(1)} %mul.94), kind=kCustom, calls=%fused_computation.24 | custom fusion | flops 262144 | bytes 1574914 | tf_op jit(solution)/shard_map/scatter | solution.py:64
  31.1 9.8 %all-to-all-start.1 = ((bf16[128,16,256]{2,1,0:T(8,128)(2,1)}), bf16[128,16,256]{2,1,0:T(8,128)(2,1)S(1)}, u32[]{:S(2)}, u32[]{:S(2)}) async-start(bf16[128,16,256]{2,1,0:T(8,128)(2,1)} %bitcast.14), calls=%async_computation.1 | async-start | bytes 2097152 | tf_op jit(solution)/shard_map/all_to_all | solution.py:68
  40.9 1.2 broadcast_in_dim.63
  42.1 5.1 %bitcast_select_fusion.1 = bf16[1,1152,2048]{2,1,0:T(8,128)(2,1)} fusion(bf16[1,1152,2048]{2,1,0:T(8,128)(2,1)} %param.10, pred[1,1152,2048]{2,1,0:T(8,128)(4,1)S(1)} %bitcast.79), kind=kLoop, calls=%fused_computation.12 | loop fusion | flops 2359296 | bytes 11796480 | tf_op jit(solution)/shard_map/jit(_where)/select_n | solution.py:33
  47.2 2.8 %bitcast_select_fusion = bf16[1152,2048]{1,0:T(8,128)(2,1)} fusion(bf16[1,1152,2048]{2,1,0:T(8,128)(2,1)S(1)} %bitcast.78, pred[72,2048]{1,0:T(8,128)(4,1)S(1)} %fusion.9), kind=kLoop, calls=%fused_computation.11 | loop fusion | flops 2359296 | bytes 9584640 | tf_op jit(solution)/shard_map/jit(_where)/select_n | solution.py:33
  50.0 0.9 all_to_all.33
  51.5 1.6 reduce.5
  53.2 6.9 %all-to-all-done.1 = bf16[128,16,256]{2,1,0:T(8,128)(2,1)S(1)} async-done(((bf16[128,16,256]{2,1,0:T(8,128)(2,1)}), bf16[128,16,256]{2,1,0:T(8,128)(2,1)S(1)}, u32[]{:S(2)}, u32[]{:S(2)}) %all-to-all-start.1) | async-done | bytes 1048608 | tf_op jit(solution)/shard_map/all_to_all | solution.py:68
  60.2 13.6 %fusion.3 = bf16[5184,256]{1,0:T(8,128)(2,1)} fusion(bf16[2048,256]{1,0:T(8,128)(2,1)S(1)} %bitcast.87, s32[2048]{0:T(1024)S(1)} %all_to_all.29), kind=kOutput, calls=%fused_computation.13 | convolution fusion | flops 5447761920 | bytes 3710976 | tf_op jit(solution)/shard_map/dot_general | solution.py:77
  73.8 4.5 %copy.33 = bf16[5184,256]{0,1:T(8,128)(2,1)} copy(bf16[5184,256]{1,0:T(8,128)(2,1)} %fusion.3) | data formatting | bytes 5308416 | tf_op jit(solution)/shard_map/convert_element_type | solution.py:80
  78.3 8.4 %reshape.225 = bf16[72,72,16,16]{1,0,3,2:T(8,128)(2,1)} reshape(bf16[5184,256]{0,1:T(8,128)(2,1)} %copy.33) | data formatting | bytes 5308416 | tf_op jit(solution)/shard_map/reshape | solution.py:80
  86.7 5.6 %copy.34 = bf16[72,16,72,16]{2,3,1,0:T(8,128)(2,1)} copy(bf16[72,16,72,16]{2,0,3,1:T(8,128)(2,1)} %bitcast.81) | data formatting | bytes 5308416 | tf_op jit(solution)/shard_map/abij,bjg->aig/dot_general | solution.py:81
  92.3 7.1 %copy.35 = bf16[1152,72,16]{0,2,1:T(8,128)(2,1)} copy(bf16[1152,72,16]{1,2,0:T(8,128)(2,1)} %bitcast.82) | data formatting | bytes 5308416 | tf_op jit(solution)/shard_map/abij,bjg->aig/dot_general | solution.py:81
  99.4 9.8 %fusion.2 = f32[2048]{0:T(1024)S(1)} fusion(bf16[1152,2048]{1,0:T(8,128)(2,1)} %bitcast_select_fusion, bf16[1152,72,16]{0,2,1:T(8,128)(2,1)} %copy.35, bf16[72,16,2048]{2,1,0:T(8,128)(2,1)} %bitcast.85), kind=kOutput, calls=%fused_computation.8 | convolution fusion | flops 5442893824 | bytes 12099584 | tf_op jit(solution)/shard_map/abij,bjg->aig/dot_general | solution.py:81
  109.5 4.6 %collective-permute-start = (f32[1,64]{1,0:T(1,128)S(1)}, f32[1,64]{1,0:T(1,128)S(1)}, u32[]{:S(2)}, u32[]{:S(2)}) collective-permute-start(f32[1,64]{1,0:T(1,128)S(1)} %get-tuple-element.5), channel_id=1, source_target_pairs={{8,0},{16,8},{24,16},{32,24},{40,32},{48,40},{56,48},{64,56},{72,6... | collective-permute-start | bytes 776 | tf_op jit(solution)/shard_map/ppermute | solution.py:23
  114.2 0.8 collective-permute-done.1
  115.1 2.3 %collective-permute-start.2 = (f32[34,1]{1,0:T(8,128)S(1)}, f32[34,1]{1,0:T(8,128)S(1)}, u32[]{:S(2)}, u32[]{:S(2)}) collective-permute-start(f32[34,1]{1,0:T(8,128)S(1)} %get-tuple-element.2), channel_id=1, source_target_pairs={{1,0},{2,1},{3,2},{4,3},{5,4},{6,5},{7,6},{0,7},{9,8},{10,9},{11,1... | collective-permute-start | bytes 416 | tf_op jit(solution)/shard_map/ppermute | solution.py:23
  117.4 1.3 collective-permute-done.2
  118.9 4.1 %multiply_convert_fusion = bf16[1,1152,2048]{2,1,0:T(8,128)(2,1)S(1)} fusion(f32[2048]{0:T(1024)S(1)} %mul.104, bf16[1,1152,2048]{2,1,0:T(8,128)(2,1)} %param.10, pred[1,1152,2048]{2,1,0:T(8,128)(4,1)S(1)} %bitcast.80), kind=kLoop, calls=%fused_computation.10 | loop fusion | flops 9437184 | bytes 11804672 | tf_op jit(solution)/shard_map/convert_element_type | solution.py:92
  123.1 15.2 %multiply_bitcast_fusion = f32[72,72,16,16]{0,3,2,1:T(8,128)} fusion(bf16[72,16,2048,1]{2,1,3,0:T(8,128)(2,1)S(1)} %bitcast.84, bf16[72,16,2048]{2,1,0:T(8,128)(2,1)} %bitcast.86), kind=kOutput, calls=%fused_computation.9 | convolution fusion | flops 5437145088 | bytes 14745600 | tf_op jit(solution)/shard_map/aig,bjg->abij/dot_general | solution.py:93
  138.3 11.7 %copy.37 = f32[72,72,16,16]{1,0,3,2:T(8,128)} copy(f32[72,72,16,16]{0,3,2,1:T(8,128)} %multiply_bitcast_fusion) | data formatting | bytes 10616832 | tf_op jit(solution)/shard_map/mul | solution.py:93
  150.0 9.1 %reshape.227 = f32[5184,256]{0,1:T(8,128)} reshape(f32[72,72,16,16]{1,0,3,2:T(8,128)} %copy.37) | data formatting | bytes 10616832 | tf_op jit(solution)/shard_map/reshape | solution.py:96
  159.1 6.1 %copy.38 = f32[5184,256]{1,0:T(8,128)} copy(f32[5184,256]{0,1:T(8,128)} %reshape.227) | data formatting | bytes 10616832 | tf_op jit(solution)/shard_map/reshape | solution.py:96
  165.2 9.1 %gather_fusion = f32[2048,256]{1,0:T(8,128)S(1)} fusion(f32[5184,256]{1,0:T(8,128)} %copy.38, s32[2048]{0:T(1024)S(1)} %broadcast_clamp_fusion), kind=kCustom, calls=%fused_computation | custom fusion | bytes 4202496 | tf_op jit(solution)/shard_map/jit(_take)/gather | solution.py:97
  174.4 1.7 broadcast_select_fusion
  176.1 9.3 %all-to-all-start.2 = ((f32[128,16,256]{2,1,0:T(8,128)}), f32[128,16,256]{2,1,0:T(8,128)S(1)}, u32[]{:S(2)}, u32[]{:S(2)}) async-start(f32[128,16,256]{2,1,0:T(8,128)} %broadcast_select_fusion), calls=%async_computation.2 | async-start | bytes 4194304 | tf_op jit(solution)/shard_map/all_to_all | solution.py:98
  185.4 30.5 %all-to-all-done.2 = f32[128,16,256]{2,1,0:T(8,128)S(1)} async-done(((f32[128,16,256]{2,1,0:T(8,128)}), f32[128,16,256]{2,1,0:T(8,128)S(1)}, u32[]{:S(2)}, u32[]{:S(2)}) %all-to-all-start.2) | async-done | bytes 2097184 | tf_op jit(solution)/shard_map/all_to_all | solution.py:98
  215.9 3.5 %gather_fusion.1 = f32[1024,256]{1,0:T(8,128)S(1)} fusion(f32[2048,256]{1,0:T(8,128)S(1)} %bitcast.76, s32[1024]{0:T(1024)S(1)} %broadcast_clamp_fusion.1), kind=kCustom, calls=%fused_computation.1 | custom fusion | bytes 2101248 | tf_op jit(solution)/shard_map/gather | solution.py:99
  220.4 0.8 fusion.19
  (87 shorter events, 9.3 us)
Async XLA Ops:
  0.6 22.7 %copy-start.4 = (s32[256,4,2]{0,2,1:T(2,128)S(1)}, s32[256,4,2]{0,2,1:T(2,128)}, u32[]{:S(2)}) copy-start(s32[256,4,2]{0,2,1:T(2,128)} %param.8) | copy-start | bytes 24580
  0.6 22.5 %copy-start.2 = (bf16[256,256]{1,0:T(8,128)(2,1)S(1)}, bf16[256,256]{1,0:T(8,128)(2,1)}, u32[]{:S(2)}) copy-start(bf16[256,256]{1,0:T(8,128)(2,1)} %param.6) | copy-start | bytes 393220
  4.7 25.8 %copy-start.5 = (s32[1024,1]{0,1:T(1,128)}, s32[1024,1]{0,1:T(1,128)S(1)}, u32[]{:S(2)}) copy-start(s32[1024,1]{0,1:T(1,128)S(1)} %compare_select_fusion.2) | copy-start | bytes 12292
  9.7 20.8 %all-to-all-start = ((s32[128,16,1]{1,2,0:T(1,128)}), s32[128,16,1]{1,2,0:T(1,128)S(1)}, u32[]{:S(2)}, u32[]{:S(2)}) async-start(s32[128,16,1]{1,2,0:T(1,128)} %bitcast.7), calls=%async_computation | async-start | bytes 131072 | tf_op jit(solution)/shard_map/all_to_all | solution.py:69
  22.8 0.7 copy-start.11
  22.8 0.7 copy-start.13
  22.8 0.6 copy-start.7
  22.9 0.6 copy-start.9
  30.5 0.6 copy-start
  31.1 29.0 %all-to-all-start.1 = ((bf16[128,16,256]{2,1,0:T(8,128)(2,1)}), bf16[128,16,256]{2,1,0:T(8,128)(2,1)S(1)}, u32[]{:S(2)}, u32[]{:S(2)}) async-start(bf16[128,16,256]{2,1,0:T(8,128)(2,1)} %bitcast.14), calls=%async_computation.1 | async-start | bytes 2097152 | tf_op jit(solution)/shard_map/all_to_all | solution.py:68
  40.9 6.3 %slice-start = ((s8[4718592]{0:T(1024)(128)(4,1)}), s8[4194304]{0:T(1024)(128)(4,1)S(1)}, s32[]{:S(2)}) async-start(s8[4718592]{0:T(1024)(128)(4,1)} %bitcast.77), calls=%async_computation.3 | async-start | bytes 8388608
  42.1 5.1 %slice-start.1 = ((s8[4718592]{0:T(1024)(128)(4,1)}), s8[524288]{0:T(1024)(128)(4,1)S(1)}, s32[]{:S(2)}) async-start(s8[4718592]{0:T(1024)(128)(4,1)} %bitcast.77), calls=%async_computation.4 | async-start | bytes 1048576
  99.4 14.7 %copy-start.1 = (s32[128,16,1]{1,2,0:T(1,128)S(1)}, s32[128,16,1]{1,2,0:T(1,128)}, u32[]{:S(2)}) copy-start(s32[128,16,1]{1,2,0:T(1,128)} %copy-done) | copy-start | bytes 24580
  109.3 5.7 %collective-permute-start.1 = (f32[1,64]{1,0:T(1,128)S(1)}, f32[1,64]{1,0:T(1,128)S(1)}, u32[]{:S(2)}, u32[]{:S(2)}) collective-permute-start(f32[1,64]{1,0:T(1,128)S(1)} %get-tuple-element.4), channel_id=1, source_target_pairs={{0,8},{8,16},{16,24},{24,32},{32,40},{40,48},{48,56},{56,64},{64,7... | collective-permute-start | bytes 776 | tf_op jit(solution)/shard_map/ppermute | solution.py:20
  109.5 5.5 %collective-permute-start = (f32[1,64]{1,0:T(1,128)S(1)}, f32[1,64]{1,0:T(1,128)S(1)}, u32[]{:S(2)}, u32[]{:S(2)}) collective-permute-start(f32[1,64]{1,0:T(1,128)S(1)} %get-tuple-element.5), channel_id=1, source_target_pairs={{8,0},{16,8},{24,16},{32,24},{40,32},{48,40},{56,48},{64,56},{72,6... | collective-permute-start | bytes 776 | tf_op jit(solution)/shard_map/ppermute | solution.py:23
  115.1 3.6 %collective-permute-start.2 = (f32[34,1]{1,0:T(8,128)S(1)}, f32[34,1]{1,0:T(8,128)S(1)}, u32[]{:S(2)}, u32[]{:S(2)}) collective-permute-start(f32[34,1]{1,0:T(8,128)S(1)} %get-tuple-element.2), channel_id=1, source_target_pairs={{1,0},{2,1},{3,2},{4,3},{5,4},{6,5},{7,6},{0,7},{9,8},{10,9},{11,1... | collective-permute-start | bytes 416 | tf_op jit(solution)/shard_map/ppermute | solution.py:23
  117.4 1.3 collective-permute-start.3
  118.8 4.2 %copy-start.3 = (f32[32,64]{1,0:T(8,128)}, f32[32,64]{1,0:T(8,128)S(1)}, u32[]{:S(2)}) copy-start(f32[32,64]{1,0:T(8,128)S(1)} %fusion.27) | copy-start | bytes 24580
  174.4 11.0 %copy-start.6 = (s32[1024,1]{0,1:T(1,128)S(1)}, s32[1024,1]{0,1:T(1,128)}, u32[]{:S(2)}) copy-start(s32[1024,1]{0,1:T(1,128)} %copy-done.5) | copy-start | bytes 12292
  176.1 39.8 %all-to-all-start.2 = ((f32[128,16,256]{2,1,0:T(8,128)}), f32[128,16,256]{2,1,0:T(8,128)S(1)}, u32[]{:S(2)}, u32[]{:S(2)}) async-start(f32[128,16,256]{2,1,0:T(8,128)} %broadcast_select_fusion), calls=%async_computation.2 | async-start | bytes 4194304 | tf_op jit(solution)/shard_map/all_to_all | solution.py:98
  215.9 4.4 %copy-start.8 = (s32[256]{0:T(256)S(1)}, s32[256]{0:T(256)}, u32[]{:S(2)}) copy-start(s32[256]{0:T(256)} %copy-done.7) | copy-start | bytes 3076
  215.9 4.4 %copy-start.10 = (s32[256]{0:T(256)S(1)}, s32[256]{0:T(256)}, u32[]{:S(2)}) copy-start(s32[256]{0:T(256)} %copy-done.9) | copy-start | bytes 3076
  215.9 4.4 %copy-start.12 = (s32[256,1]{0,1:T(1,128)S(1)}, s32[256,1]{0,1:T(1,128)}, u32[]{:S(2)}) copy-start(s32[256,1]{0,1:T(1,128)} %copy-done.11) | copy-start | bytes 3076
  215.9 4.4 %copy-start.14 = (s32[256,1]{0,1:T(1,128)S(1)}, s32[256,1]{0,1:T(1,128)}, u32[]{:S(2)}) copy-start(s32[256,1]{0,1:T(1,128)} %copy-done.13) | copy-start | bytes 3076
where the time goes:
time: 223 us; the launch traced here: 221 us
  local copies, waits for them, and re-layouts  78.2 us (35%)
  waiting for transfers between devices  39.5 us (18%)
  matrix products  38.7 us (17%)
  starting transfers between devices  37.7 us (17%)
  other arithmetic  26.1 us (12%)
    all_to_all x1, waiting for transfers between devices, shards(): lax.all_to_all(partial_blocks, ('gx', 'gy'), split_axis=0, concat_axis=0,...  30.5 us
    dot_general x1, matrix products, shards(): jnp.einsum('aig,bjg->abij', basis_three, weighted, preferred_element_type...  15.2 us
    reshape x2, local copies, waits for them, and re-layouts, shards(): flat_blocks = hamilton.reshape(atom_slots * atom_slots, width * width)  15.2 us
    dot_general x1, matrix products, shards(): lax.dot_general(code_table, got_blocks, (((0,), (0,)), ((), ())), preferr...  13.6 us
    dot_general x2, local copies, waits for them, and re-layouts, shards(): jnp.einsum('abij,bjg->aig', matrix, basis_three, preferred_element_type=j...  12.7 us
    mul x1, local copies, waits for them, and re-layouts, shards(): jnp.einsum('aig,bjg->abij', basis_three, weighted, preferred_element_type...  11.7 us
    all_to_all x1, starting transfers between devices, shards(): lax.all_to_all(send_codes, ('gx', 'gy'), split_axis=0, concat_axis=0, til...  11.5 us
    dot_general x1, matrix products, shards(): jnp.einsum('abij,bjg->aig', matrix, basis_three, preferred_element_type=j...  9.82 us
  transfers between devices with their start and end apart: 7, of which 4 were waited for; matrix products, arithmetic and copies ran while one was open for 9% of the time, Pallas kernels for 0%

commit v1 on v0

v1 whole, which is shorter than its diff:
```python
import functools

import jax
import jax.numpy as jnp
from jax import lax
from jax.experimental import pallas as pl
from jax.experimental.pallas import tpu as pltpu
from jax.sharding import PartitionSpec as P

NB = 16
CX = 32
CY = 64
LANES = 128
GROUPS = LANES // NB
WIDTH = NB * NB
CAP = 16
BATCH = 16
MESH = pl.DeviceIdType.MESH
F32 = jnp.float32
BF16 = jnp.bfloat16
I32 = jnp.int32
VMEM_BYTES = 60 * 1024 * 1024
gradient_weight = 1.0
NT = (((1,), (1,)), ((), ()))


def iota(shape, dim):
    return lax.broadcasted_iota(I32, shape, dim)


def dot(a, b, dims=(((1,), (0,)), ((), ()))):
    return lax.dot_general(a, b, dims, preferred_element_type=F32)


def ones_where(condition):
    return jnp.where(condition, 1.0, 0.0)


def size_mask_of(sizes):
    pairs = sizes.shape[1]
    eye = ones_where(iota((pairs, pairs), 0) == iota((pairs, pairs), 1)).astype(BF16)
    wide = sizes.astype(F32)
    first = dot(eye, jnp.broadcast_to(wide[0:1], (WIDTH, pairs)).astype(BF16), NT)
    second = dot(eye, jnp.broadcast_to(wide[1:2], (WIDTH, pairs)).astype(BF16), NT)
    lane = iota((pairs, WIDTH), 1)
    row = (lane // NB).astype(F32)
    col = (lane % NB).astype(F32)
    return (row < first) & (col < second)


def key_offset(column_tile):
    half = column_tile // 2
    return 16 * (half + 1) * (half + column_tile % 2)


def turned():
    row, lane = iota((WIDTH, WIDTH), 0), iota((WIDTH, WIDTH), 1)
    return ones_where((row // NB == lane % NB) & (row % NB == lane // NB)).astype(BF16)


def pack(tiles, slots_ref, masked, chunks, codes, picks):
    targets, pairs = tiles.shape
    devices = chunks.shape[0]
    tile_id = iota((devices, pairs), 0)
    chosen = jnp.zeros((devices, pairs), F32)
    kind = jnp.zeros((devices, pairs), F32)
    asked = []
    for k in range(targets):
        mark = ones_where(tiles[k : k + 1] == tile_id)
        slots = slots_ref[k].astype(F32)
        first, second = slots[0:1], slots[1:2]
        chosen = chosen + mark
        kind = kind + mark * (ones_where(first < second) + 2.0 * ones_where(first > second))
        asked += [tiles[k : k + 1].astype(F32), jnp.minimum(first, second), jnp.maximum(first, second)]
    asked = jnp.concatenate(asked + [jnp.zeros((16 - 3 * targets, pairs), F32)], axis=0).astype(BF16)
    before = ones_where(iota((pairs, pairs), 0) < iota((pairs, pairs), 1)).astype(BF16)
    rank = dot(chosen.astype(BF16), before)
    marked = jnp.where(chosen > 0.5, rank * 4.0 + kind, -4.0)
    blocks = jnp.concatenate([masked, dot(masked, turned()).astype(BF16)], axis=0)
    step = 32
    own = (4 * (iota((step * CAP, pairs), 0) % CAP)).astype(F32)
    for start in range(0, devices, step):
        rows = jnp.broadcast_to(marked[start : start + step, None, :], (step, CAP, pairs))
        rows = rows.reshape(step * CAP, pairs) - own
        same, upper, lower = ones_where(rows == 0.0), ones_where(rows == 1.0), ones_where(rows == 2.0)
        straight = (same + upper).astype(BF16)
        across = lower.astype(BF16)
        here = slice(start * CAP, (start + step) * CAP)
        picks[here, :pairs] = straight
        picks[here, pairs:] = across
        weights = jnp.concatenate([(same + 2.0 * upper).astype(BF16), (2.0 * lower).astype(BF16)], axis=1)
        chunks[start : start + step] = dot(weights, blocks).astype(BF16).reshape(step, CAP, WIDTH)
        told = dot(asked, straight + across, NT)
        tile = (start + iota((1, step * CAP), 1) // CAP).astype(F32)
        first = jnp.zeros((1, step * CAP), F32)
        second = jnp.zeros((1, step * CAP), F32)
        for k in range(targets):
            hit = told[3 * k : 3 * k + 1] == tile
            first = first + jnp.where(hit, told[3 * k + 1 : 3 * k + 2], 0.0)
            second = second + jnp.where(hit, told[3 * k + 2 : 3 * k + 3], 0.0)
        column_tile = jnp.floor(second * (1.0 / GROUPS))
        half = jnp.floor(column_tile * 0.5)
        key = 16.0 * (half + 1.0) * (column_tile - half) + first
        code = key * GROUPS + (second - column_tile * GROUPS)
        for n in range(step * CAP // LANES):
            codes[start * CAP // LANES + n] = code[:, n * LANES : (n + 1) * LANES]


INNER = [(j % 4, (j // 4 + j) % 4, (j + 3 * (j // 4)) % 4) for j in range(BATCH)]


def places(b, gx, gy, outward):
    core = gy % 2
    other = (core + b % 2) % 2
    turn = 1 + 2 * core if outward else 3 - 2 * other
    x, y, z = gx // 4, gx % 4, gy // 2
    xs = [((x + d * turn) % 4) * 4 for d in range(4)]
    ys = [(y + d * turn) % 4 for d in range(4)]
    zs = [((z + (b // 2 + d) * turn) % 4) * 2 + other for d in range(4)]
    return [(xs[dx] + ys[dy], zs[dz]) for dx, dy, dz in INNER]


def remote(source, target, send_sem, recv_sem, place):
    return pltpu.make_async_remote_copy(
        src_ref=source, dst_ref=target, send_sem=send_sem, recv_sem=recv_sem, device_id=place, device_id_type=MESH,
    )


def mask_basis(basis, extent):
    functions, cells = basis.shape
    atoms = functions // NB
    extent = extent.astype(F32)
    own = ones_where(iota((functions, atoms), 0) // NB == iota((functions, atoms), 1)).astype(BF16)
    half = (iota((functions, LANES), 1) // CY).astype(F32)
    low = dot(own, jnp.broadcast_to(extent[0:1], (LANES, atoms)).astype(BF16), NT) - half
    high = dot(own, jnp.broadcast_to(extent[1:2], (LANES, atoms)).astype(BF16), NT) - half
    for c in range(cells // LANES):
        row = float(c * (LANES // CY))
        inside = ones_where((low <= row) & (high > row)).astype(BF16)
        lanes = slice(c * LANES, (c + 1) * LANES)
        basis[:, lanes] = basis[:, lanes] * inside


def fill_spread(spread, fold):
    wide = 2 * LANES
    for c in range(NB // 2):
        row, lane = iota((WIDTH, wide), 0), iota((WIDTH, wide), 1)
        same = (row // NB == 2 * c + lane // LANES) & (row % NB == lane % NB)
        spread[:, c * wide : (c + 1) * wide] = ones_where(same).astype(BF16)
        row, lane = iota((wide, WIDTH), 0), iota((wide, WIDTH), 1)
        same = (lane // NB == 2 * c + row // LANES) & (lane % NB == row % NB)
        fold[c * wide : (c + 1) * wide, :] = ones_where(same).astype(BF16)


def collect(recv, got, b, lane_group, spread, gathered, keys, groups):
    entries = BATCH * CAP
    codes = got[pl.ds(b * BATCH, BATCH), 0, :]
    key = jnp.floor(codes * (1.0 / GROUPS))
    group = (codes - key * GROUPS).astype(BF16)
    coarse = jnp.floor(key * (1.0 / 16.0)) * 16.0
    fine = (key - coarse).astype(BF16)
    coarse = coarse.astype(BF16)
    row, lane = iota((LANES, entries), 0), iota((LANES, entries), 1)
    own = ones_where(row == lane_group * CAP + lane % CAP).astype(BF16)
    keyed = dot(fine, own) + dot(coarse, own)
    keyed = jnp.where(iota((BATCH, entries), 0) == iota((BATCH, entries), 1) // CAP, keyed, 0.0)
    key_row = jnp.sum(keyed, axis=0, keepdims=True).astype(I32)
    key_rows = gathered.shape[0]
    onehot = ones_where(iota((key_rows, entries), 0) == key_row).astype(BF16)
    slot = ones_where(iota((entries, BATCH), 0) // CAP == iota((entries, BATCH), 1)).astype(BF16)
    row, lane = iota((entries, LANES), 0), iota((entries, LANES), 1)
    own = lane == lane_group * CAP + row % CAP
    every = jnp.ones((LANES, LANES), BF16)
    parts = [jnp.where(own, dot(slot, part), 0.0).astype(BF16) for part in (fine, coarse, group)]
    key = dot(parts[0], every) + dot(parts[1], every)
    group = dot(parts[2], every)
    here = pl.ds(pl.multiple_of(b * entries, entries), entries)
    keys[here, :] = key
    groups[here, :] = group
    blocks = recv[pl.ds(b * BATCH, BATCH)].reshape(entries, WIDTH)
    wide = 2 * LANES
    inside = (iota((entries, wide), 1) % LANES // NB).astype(F32) == jnp.concatenate([group, group], axis=1)
    for c in range(NB // 2):
        lanes = slice(c * wide, (c + 1) * wide)
        spaced = jnp.where(inside, dot(blocks, spread[:, lanes]), 0.0).astype(BF16)
        gathered[:, lanes] = gathered[:, lanes] + dot(onehot, spaced)


def pick(b, picked, keys, groups, fold, spaced, back):
    entries = BATCH * CAP
    here = pl.ds(pl.multiple_of(b * entries, entries), entries)
    key, group = keys[here, :], groups[here, :]
    lane = iota((entries, LANES), 1).astype(F32)
    onehot = jnp.concatenate(
        [ones_where(lane + float(n * LANES) == key).astype(BF16) for n in range(picked.shape[0] // LANES)], axis=1
    )
    wide = 2 * LANES
    inside = (iota((entries, wide), 1) % LANES // NB).astype(F32) == jnp.concatenate([group, group], axis=1)
    for c in range(NB // 2):
        lanes = slice(c * wide, (c + 1) * wide)
        spaced[:, lanes] = jnp.where(inside, dot(onehot, picked[:, lanes]), 0.0).astype(BF16)
    blocks = dot(spaced[...], fold[...]).astype(BF16)
    back[pl.ds(b * BATCH, BATCH)] = blocks.reshape(BATCH, CAP, WIDTH)


def potential_of(charge, below, above, left, right):
    rows = charge.shape[0]
    lane = iota((rows, LANES), 1)
    row = iota((rows, LANES), 0)
    swapped = pltpu.roll(charge, CY, 1)
    first_of_above = pltpu.roll(above, CY, 1)[0:1]
    last_of_below = pltpu.roll(below, CY, 1)[rows - 1 : rows]
    up = jnp.where(row == rows - 1, first_of_above, pltpu.roll(swapped, rows - 1, 0))
    next_x = jnp.where(lane < CY, swapped, up)
    down = jnp.where(row == 0, last_of_below, pltpu.roll(swapped, 1, 0))
    last_x = jnp.where(lane < CY, down, swapped)
    next_y = jnp.where(lane % CY == CY - 1, pltpu.roll(right, CY - 1, 1), pltpu.roll(charge, LANES - 1, 1))
    last_y = jnp.where(lane % CY == 0, pltpu.roll(left, LANES - CY + 1, 1), pltpu.roll(charge, 1, 1))
    slope_x = 0.5 * (next_x - last_x)
    slope_y = 0.5 * (next_y - last_y)
    return charge * lax.rsqrt(
        1.0 + charge * charge + gradient_weight * (slope_x * slope_x + slope_y * slope_y)
    )


def whole_kernel(
    tiles_hbm, slots_hbm, sizes_hbm, density_hbm, extent_hbm, basis_hbm,
    out_hbm, potential_hbm,
    tiles_ref, slots_ref, sizes_ref, density_ref, extent_ref, out_ref, potential_ref,
    basis, weighted, chunks, recv, back, returned, codes, got, picks, picks_turned, spread, fold, gathered, keys, groups,
    square, matrix, picked, spaced, charge, halo,
    send_sems, recv_sems, code_sems, return_sem, halo_send, halo_recv, local_sem,
):
    devices = chunks.shape[0]
    functions, cells = basis.shape
    atoms = functions // NB
    column_tiles = functions // LANES
    batches = devices // BATCH
    gx, gy = lax.axis_index("gx"), lax.axis_index("gy")
    me = gx * 8 + gy
    load = pltpu.make_async_copy(basis_hbm, basis, local_sem.at[0])
    inputs = [
        pltpu.make_async_copy(source, target, local_sem.at[1 + n])
        for n, (source, target) in enumerate((
            (tiles_hbm, tiles_ref), (slots_hbm, slots_ref), (sizes_hbm, sizes_ref), (density_hbm, density_ref),
            (extent_hbm, extent_ref),
        ))
    ]
    for copy in inputs:
        copy.start()
    load.start()
    barrier = pltpu.get_barrier_semaphore()

    def greet(b, carry):
        for j, place in enumerate(places(b, gx, gy, True)):
            def signal():
                pl.semaphore_signal(barrier, inc=1, device_id=place, device_id_type=MESH)

            if j == 0:
                pl.when(b > 0)(signal)
            else:
                signal()
        return carry

    lax.fori_loop(0, batches, greet, 0)
    for copy in inputs:
        copy.wait()
    mask = size_mask_of(sizes_ref[...])
    masked = jnp.where(mask, density_ref[...].astype(F32), 0.0).astype(BF16)
    pack(tiles_ref[...], slots_ref, masked, chunks, codes, picks)
    pl.semaphore_wait(barrier, devices - 1)
    tiles_per_row = LANES // CAP
    pltpu.make_async_copy(codes.at[me // tiles_per_row], got.at[0], code_sems.at[0]).start()
    pltpu.make_async_copy(chunks.at[me], recv.at[0], recv_sems.at[0]).start()

    def push(b, carry):
        for j, (px, py) in enumerate(places(b, gx, gy, True)):
            def start():
                slot = b * BATCH + j
                remote(codes.at[px], got.at[slot], send_sems.at[0], code_sems.at[b], (px, py)).start()
                remote(chunks.at[px * 8 + py], recv.at[slot], send_sems.at[1], recv_sems.at[b], (px, py)).start()

            if j == 0:
                pl.when(b > 0)(start)
            else:
                start()
        return carry

    lax.fori_loop(0, batches, push, 0)
    pairs = density_ref.shape[0]
    for half in range(2):
        for n in range(devices * CAP // 512):
            part = picks[n * 512 : (n + 1) * 512, half * pairs : (half + 1) * pairs].astype(F32)
            lanes = half * devices * CAP + n * 512
            picks_turned[:, lanes : lanes + 512] = jnp.transpose(part).astype(BF16)
    square[...] = jnp.zeros_like(square)
    fill_spread(spread, fold)
    gathered[...] = jnp.zeros_like(gathered)
    picked[...] = jnp.zeros_like(picked)
    load.wait()
    mask_basis(basis, extent_ref[...])

    def arrive(b, carry):
        slots = pl.ds(b * BATCH, BATCH)
        remote(got.at[slots], got.at[slots], send_sems.at[0], code_sems.at[b], (gx, gy)).wait_recv()
        remote(recv.at[slots], recv.at[slots], send_sems.at[1], recv_sems.at[b], (gx, gy)).wait_recv()
        collect(recv, got, b, gy, spread, gathered, keys, groups)
        return carry

    lax.fori_loop(0, batches, arrive, 0)
    for c in range(column_tiles):
        low = key_offset(c)
        count = GROUPS * (c + 1)
        for i in range(NB):
            block = gathered[low : low + count, i * LANES : (i + 1) * LANES]
            square[c, pl.ds(i, count, stride=NB), :] = block
        matrix[:, c * LANES : (c + 1) * LANES] = square[c].astype(BF16)
    step = 2 * LANES
    part = 3 * LANES
    for c in range(cells // step):
        columns = basis[:, c * step : (c + 1) * step]
        total = jnp.zeros((1, step), F32)
        for low in range(0, functions, part):
            product = dot(matrix[low : low + part, low:], columns[low:])
            product = product * columns[low : low + part].astype(F32)
            total = total + jnp.sum(product, axis=0, keepdims=True)
        charge[2 * c : 2 * c + 1, :] = total[:, :LANES]
        charge[2 * c + 1 : 2 * c + 2, :] = total[:, LANES:]
    edges = [
        remote(charge, halo.at[n], halo_send.at[n], halo_recv.at[n], place)
        for n, place in enumerate(
            (((gx + 1) % 16, gy), ((gx + 15) % 16, gy), (gx, (gy + 7) % 8), (gx, (gy + 1) % 8))
        )
    ]
    for copy in edges:
        copy.start()
    for copy in edges:
        copy.wait()
    potential = potential_of(charge[...], halo[0], halo[1], halo[3], halo[2])
    for half in range(2):
        rows = potential if half == 0 else pltpu.roll(potential, CY, 1)
        potential_ref[pl.ds(half, CX // 2, stride=2), :] = rows[:, :CY]
    potential_out = pltpu.make_async_copy(potential_ref, potential_hbm, local_sem.at[1])
    potential_out.start()
    for c in range(cells // LANES):
        lanes = slice(c * LANES, (c + 1) * LANES)
        weighted[:, lanes] = (basis[:, lanes].astype(F32) * potential[c : c + 1]).astype(BF16)
    for start in range(0, column_tiles, 2):
        stop = min(start + 2, column_tiles)
        rows = weighted[start * LANES : stop * LANES, :]
        high = stop * LANES
        product = dot(basis[:high, :], rows, NT) * float(cells) ** -0.5
        for c in range(start, stop):
            square[c, :high, :] = product[:, (c - start) * LANES : (c - start + 1) * LANES]
            low = key_offset(c)
            count = GROUPS * (c + 1)
            for i in range(NB):
                block = square[c, pl.ds(i, count, stride=NB), :]
                picked[low : low + count, i * LANES : (i + 1) * LANES] = block.astype(BF16)
    keep = pltpu.make_async_copy(back.at[0], returned.at[me], return_sem)

    def give(b, carry):
        pick(b, picked, keys, groups, fold, spaced, back)

        for j, place in enumerate(places(b, gx, gy, False)):
            def start():
                remote(back.at[b * BATCH + j], returned.at[me], send_sems.at[2], return_sem, place).start()

            if j == 0:
                pl.when(b > 0)(start)
                pl.when(b == 0)(keep.start)
            else:
                start()
        return carry

    lax.fori_loop(0, batches, give, 0)
    remote(returned, returned, send_sems.at[2], return_sem, (gx, gy)).wait_recv()
    blocks = returned[...].reshape(devices * CAP, WIDTH)
    blocks = jnp.concatenate([blocks, dot(blocks, turned()).astype(BF16)], axis=0)
    out_ref[...] = jnp.where(size_mask_of(sizes_ref[...]), dot(picks_turned[...], blocks), 0.0)
    out = pltpu.make_async_copy(out_ref, out_hbm, local_sem.at[2])
    out.start()
    out.wait()
    potential_out.wait()
    others = pl.ds(0, devices - 1)
    remote(got.at[others], got.at[others], send_sems.at[0], code_sems.at[0], (gx, gy)).wait_send()
    remote(chunks.at[others], recv.at[others], send_sems.at[1], recv_sems.at[0], (gx, gy)).wait_send()
    remote(back.at[others], returned.at[others], send_sems.at[2], return_sem, (gx, gy)).wait_send()


def finish_kernel(summed, field, out, potential, sems):
    copies = [
        pltpu.make_async_copy(source, target, sems.at[n])
        for n, (source, target) in enumerate(((summed, out), (field, potential)))
    ]
    for copy in copies:
        copy.start()
    for copy in copies:
        copy.wait()


ANY_SPEC = pl.BlockSpec(memory_space=pl.ANY)
DMA = pltpu.SemaphoreType.DMA


def shards(density, pair_tiles, pair_slots, pair_sizes, basis_table, tile_extent):
    devices = lax.axis_size("gx") * lax.axis_size("gy")
    pairs, targets = pair_tiles.shape
    atoms = tile_extent.shape[2]
    functions, cells = basis_table.shape[1:]
    rows = cells // LANES
    key_rows = key_offset(functions // LANES)
    chunk = pltpu.VMEM((devices, CAP, WIDTH), BF16)
    entries = devices * CAP
    spaced = NB * LANES
    results = pl.pallas_call(
        whole_kernel,
        name="whole",
        out_shape=[
            jax.ShapeDtypeStruct((pairs, WIDTH), F32),
            jax.ShapeDtypeStruct((CX, CY), F32),
        ],
        in_specs=[ANY_SPEC] * 6,
        out_specs=[ANY_SPEC] * 2,
        scratch_shapes=[
            pltpu.VMEM((targets, pairs), I32),
            pltpu.VMEM((targets, 2, pairs), I32),
            pltpu.VMEM((2, pairs), I32),
            pltpu.VMEM((pairs, WIDTH), BF16),
            pltpu.VMEM((2, atoms), I32),
            pltpu.VMEM((pairs, WIDTH), F32),
            pltpu.VMEM((CX, CY), F32),
            pltpu.VMEM((functions, cells), BF16),
            pltpu.VMEM((functions, cells), BF16),
            chunk,
            chunk,
            chunk,
            chunk,
            pltpu.VMEM((devices * CAP // LANES, 1, LANES), F32),
            pltpu.VMEM((devices, 1, LANES), F32),
            pltpu.VMEM((entries, 2 * pairs), BF16),
            pltpu.VMEM((pairs, 2 * entries), BF16),
            pltpu.VMEM((WIDTH, spaced), BF16),
            pltpu.VMEM((spaced, WIDTH), BF16),
            pltpu.VMEM((key_rows, spaced), F32),
            pltpu.VMEM((entries, LANES), F32),
            pltpu.VMEM((entries, LANES), F32),
            pltpu.VMEM((functions // LANES, functions, LANES), F32),
            pltpu.VMEM((functions, functions), BF16),
            pltpu.VMEM((-(-key_rows // LANES) * LANES, spaced), BF16),
            pltpu.VMEM((BATCH * CAP, spaced), BF16),
            pltpu.VMEM((rows, LANES), F32),
            pltpu.VMEM((4, rows, LANES), F32),
            DMA((3,)),
            DMA((devices // BATCH,)),
            DMA((devices // BATCH,)),
            DMA,
            DMA((4,)),
            DMA((4,)),
            DMA((6,)),
        ],
        compiler_params=pltpu.CompilerParams(
            vmem_limit_bytes=VMEM_BYTES, collective_id=1, has_side_effects=True
        ),
    )(pair_tiles.T, pair_slots.transpose(1, 2, 0), pair_sizes.T, density, tile_extent[0], basis_table[0])
    return tuple(pl.pallas_call(
        finish_kernel,
        name="finish",
        out_shape=[jax.ShapeDtypeStruct(result.shape, result.dtype) for result in results],
        in_specs=[ANY_SPEC] * 2,
        out_specs=[ANY_SPEC] * 2,
        scratch_shapes=[DMA((2,))],
        compiler_params=pltpu.CompilerParams(vmem_limit_bytes=VMEM_BYTES),
    )(*results))


def solution(mesh):
    in_specs = (
        P(("gx", "gy"), None),
        P(("gx", "gy"), None),
        P(("gx", "gy"), None, None),
        P(("gx", "gy"), None),
        P(("gx", "gy"), None, None),
        P(("gx", "gy"), None, None),
    )
    out_specs = (P(("gx", "gy"), None), P("gx", "gy"))
    return jax.shard_map(shards, mesh=mesh, in_specs=in_specs, out_specs=out_specs, check_vma=False)
```

time: 223 us -> 74.3 us (0.33)
  local copies, waits for them, and re-layouts: 78.2 us -> 0 us
  Pallas kernels: 0 us -> 73.4 us
  waiting for transfers between devices: 39.5 us -> 0 us
  matrix products: 38.7 us -> 0 us
  starting transfers between devices: 37.7 us -> 0 us
  other arithmetic: 26.1 us -> 0 us
    pallas_call x0 -> x2, Pallas kernels: none -> 73.4 us  [the longest x1 63.8 us: shards(): pl.pallas_call(whole_kernel, name='whole', out_shape=[jax.ShapeDtypeStruc...]
    dot_general x3 -> x0, matrix products: 38.7 us -> none  [the longest x1 15.2 us: shards(): jnp.einsum('aig,bjg->abij', basis_three, weighted, preferred_element_type...]
    all_to_all x3 -> x0, waiting for transfers between devices: 37.4 us -> none  [the longest x1 30.5 us: shards(): lax.all_to_all(partial_blocks, ('gx', 'gy'), split_axis=0, concat_axis=0,...]
    all_to_all x3 -> x0, starting transfers between devices: 30.6 us -> none  [the longest x1 11.5 us: shards(): lax.all_to_all(send_codes, ('gx', 'gy'), split_axis=0, concat_axis=0, til...]
    reshape x5 -> x0, local copies, waits for them, and re-layouts: 24 us -> none  [the longest x2 15.2 us: shards(): flat_blocks = hamilton.reshape(atom_slots * atom_slots, width * width)]
    dot_general x2 -> x0, local copies, waits for them, and re-layouts: 12.7 us -> none  [shards(): jnp.einsum('abij,bjg->aig', matrix, basis_three, preferred_element_type=j...]
    gather x2 -> x0, local copies, waits for them, and re-layouts: 12.6 us -> none  [the longest x1 9.14 us: shards(): partial_blocks = jnp.take(flat_blocks, got_codes, axis=0)]
    mul x7 -> x0, local copies, waits for them, and re-layouts: 12.4 us -> none  [the longest x1 11.7 us: shards(): jnp.einsum('aig,bjg->abij', basis_three, weighted, preferred_element_type...]
  transfers between devices with their start and end apart: 7 -> 0, of which waited for: 4 -> 0; matrix products, arithmetic and copies ran while one was open for 9% -> 0% of each run, Pallas kernels for 0% -> 0%
where the time goes in v1:
time: 74.3 us; the launch traced here: 74.2 us
  Pallas kernels  73.4 us (99%)
  between operations  0.8 us (1%)
    pallas_call x1, Pallas kernels, shards(): pl.pallas_call(whole_kernel, name='whole', out_shape=[jax.ShapeDtypeStruc...  63.8 us
    pallas_call x1, Pallas kernels, shards(): pl.pallas_call(finish_kernel, name='finish', out_shape=[jax.ShapeDtypeStr...  9.56 us

profile of v1, /device:TPU:1, one launch (start us, length us, event | category | flops | bytes accessed | tf_op | source)
XLA Modules:
  0.0 74.2 jit_solution(3793588436496887325)
XLA Ops:
  0.6 63.8 %whole.1 = (f32[256,256]{1,0:T(8,128)}, f32[32,64]{1,0:T(8,128)}) custom-call(s32[4,256]{1,0:T(4,128)} %bitcast.7, s32[4,2,256]{2,1,0:T(2,128)} %bitcast.6, s32[2,256]{1,0:T(2,128)} %bitcast.8, bf16[256,256]{1,0:T(8,128)(2,1)} %density_hbm.1, s32[2,72]{1,0:T(2,128)} %bitcast.9, bf16[1152,2048]{1,0:T(8,128)(2,1)} %bitcast.5), custom_call_target="tpu_custom_call" | custom-call | tf_op jit(solution)/shard_map/whole/pallas_call | solution.py:416
  64.5 9.6 %finish.1 = (f32[256,256]{1,0:T(8,128)}, f32[32,64]{1,0:T(8,128)}) custom-call(f32[256,256]{1,0:T(8,128)} %get-tuple-element.4.summed, f32[32,64]{1,0:T(8,128)} %get-tuple-element.5.field), custom_call_target="tpu_custom_call" | custom-call | tf_op jit(solution)/shard_map/finish/pallas_call | solution.py:466

commit v2 on v1

v2 whole, which is shorter than its diff:
```python
import functools

import jax
import jax.numpy as jnp
import numpy as np
from jax import lax
from jax.experimental import pallas as pl
from jax.experimental.pallas import tpu as pltpu
from jax.sharding import PartitionSpec as P

NB = 16
CX = 32
CY = 64
LANES = 128
GROUPS = LANES // NB
WIDTH = NB * NB
CAP = 16
BATCH = 16
STEP = 32
MESH = pl.DeviceIdType.MESH
F32 = jnp.float32
BF16 = jnp.bfloat16
I32 = jnp.int32
VMEM_BYTES = 60 * 1024 * 1024
gradient_weight = 1.0
NT = (((1,), (1,)), ((), ()))


def iota(shape, dim):
    return lax.broadcasted_iota(I32, shape, dim)


def dot(a, b, dims=(((1,), (0,)), ((), ()))):
    return lax.dot_general(a, b, dims, preferred_element_type=F32)


def ones_where(condition):
    return jnp.where(condition, 1.0, 0.0)


def size_mask_of(sizes, eye):
    pairs = sizes.shape[1]
    wide = sizes.astype(F32)
    first = dot(eye, jnp.broadcast_to(wide[0:1], (WIDTH, pairs)).astype(BF16), NT)
    second = dot(eye, jnp.broadcast_to(wide[1:2], (WIDTH, pairs)).astype(BF16), NT)
    lane = iota((pairs, WIDTH), 1)
    row = (lane // NB).astype(F32)
    col = (lane % NB).astype(F32)
    return (row < first) & (col < second)


def key_offset(column_tile):
    half = column_tile // 2
    return 16 * (half + 1) * (half + column_tile % 2)


def plan(tiles, slots_ref, tile_id, before, marks):
    targets, pairs = tiles.shape
    devices = marks.shape[0]
    chosen = jnp.zeros((devices, pairs), F32)
    kind = jnp.zeros((devices, pairs), F32)
    asked = []
    for k in range(targets):
        mark = ones_where(tiles[k : k + 1] == tile_id)
        slots = slots_ref[k].astype(F32)
        first, second = slots[0:1], slots[1:2]
        chosen = chosen + mark
        kind = kind + mark * (ones_where(first < second) + 2.0 * ones_where(first > second))
        asked += [tiles[k : k + 1].astype(F32), jnp.minimum(first, second), jnp.maximum(first, second)]
    rank = dot(chosen.astype(BF16), before)
    marks[...] = jnp.where(chosen > 0.5, rank * 4.0 + kind, -4.0)
    return jnp.concatenate(asked + [jnp.zeros((16 - 3 * targets, pairs), F32)], axis=0).astype(BF16)


def pack(b, tile, asked, blocks, marks, chunks, codes, picks):
    pairs = marks.shape[1]
    entries = STEP * CAP
    own = (4 * (iota((entries, pairs), 0) % CAP)).astype(F32)
    rows = jnp.broadcast_to(marks[pl.ds(b * STEP, STEP), :][:, None, :], (STEP, CAP, pairs))
    rows = rows.reshape(entries, pairs) - own
    same, upper, lower = ones_where(rows == 0.0), ones_where(rows == 1.0), ones_where(rows == 2.0)
    straight = (same + upper).astype(BF16)
    across = lower.astype(BF16)
    here = pl.ds(pl.multiple_of(b * entries, entries), entries)
    picks[here, :pairs] = straight
    picks[here, pairs:] = across
    weights = jnp.concatenate([(same + 2.0 * upper).astype(BF16), (2.0 * lower).astype(BF16)], axis=1)
    chunks[pl.ds(b * STEP, STEP)] = dot(weights, blocks).astype(BF16).reshape(STEP, CAP, WIDTH)
    told = dot(asked, straight + across, NT)
    first = jnp.zeros((1, entries), F32)
    second = jnp.zeros((1, entries), F32)
    for k in range(asked.shape[0] // 3):
        hit = told[3 * k : 3 * k + 1] == tile
        first = first + jnp.where(hit, told[3 * k + 1 : 3 * k + 2], 0.0)
        second = second + jnp.where(hit, told[3 * k + 2 : 3 * k + 3], 0.0)
    column_tile = jnp.floor(second * (1.0 / GROUPS))
    half = jnp.floor(column_tile * 0.5)
    key = 16.0 * (half + 1.0) * (column_tile - half) + first
    code = key * GROUPS + (second - column_tile * GROUPS)
    for n in range(entries // LANES):
        codes[b * (entries // LANES) + n] = code[:, n * LANES : (n + 1) * LANES]


INNER = [(j % 4, (j // 4 + j) % 4, (j + 3 * (j // 4)) % 4) for j in range(BATCH)]


def places(b, gx, gy, outward):
    core = gy % 2
    other = (core + b % 2) % 2
    turn = 1 + 2 * core if outward else 3 - 2 * other
    x, y, z = gx // 4, gx % 4, gy // 2
    xs = [((x + d * turn) % 4) * 4 for d in range(4)]
    ys = [(y + d * turn) % 4 for d in range(4)]
    zs = [((z + (b // 2 + d) * turn) % 4) * 2 + other for d in range(4)]
    return [(xs[dx] + ys[dy], zs[dz]) for dx, dy, dz in INNER]


def tile_of(slot, gx, gy):
    b, j = slot >> 4, slot & 15
    dx, dy, dz = j & 3, ((j >> 2) + j) & 3, ((b >> 1) + j + 3 * (j >> 2)) & 3
    core = gy % 2
    turn = 1 + 2 * core
    px = ((gx // 4 + dx * turn) & 3) * 4 + ((gx % 4 + dy * turn) & 3)
    return px * 8 + ((gy // 2 + dz * turn) & 3) * 2 + ((core + b) & 1)


def remote(source, target, send_sem, recv_sem, place):
    return pltpu.make_async_remote_copy(
        src_ref=source, dst_ref=target, send_sem=send_sem, recv_sem=recv_sem, device_id=place, device_id_type=MESH,
    )


def mask_basis(basis, extent):
    functions, cells = basis.shape
    atoms = functions // NB
    extent = extent.astype(F32)
    own = ones_where(iota((functions, atoms), 0) // NB == iota((functions, atoms), 1)).astype(BF16)
    half = (iota((functions, LANES), 1) // CY).astype(F32)
    low = dot(own, jnp.broadcast_to(extent[0:1], (LANES, atoms)).astype(BF16), NT) - half
    high = dot(own, jnp.broadcast_to(extent[1:2], (LANES, atoms)).astype(BF16), NT) - half
    for c in range(cells // LANES):
        row = c * (LANES // CY)
        inside = low <= float(row) if row < CX // 2 else high > float(row)
        lanes = slice(c * LANES, (c + 1) * LANES)
        basis[:, lanes] = basis[:, lanes] * ones_where(inside).astype(BF16)


def constants():
    row, lane = np.arange(WIDTH)[:, None], np.arange(WIDTH)[None, :]
    before = row < lane
    turned = (row // NB == lane % NB) & (row % NB == lane // NB)
    wide = np.arange(NB * LANES)[None, :]
    spread = (row // NB == wide // LANES) & (row % NB == wide % NB)
    square = np.concatenate([before, turned, row == lane], axis=1)
    return [np.asarray(x, np.float32) for x in (square, spread, spread.T)]


def collect(recv, got, b, spread, gathered, keys, groups):
    entries = STEP * CAP
    codes = got[pl.ds(b * STEP, STEP), 0, :]
    key = jnp.floor(codes * (1.0 / GROUPS))
    group = (codes - key * GROUPS).astype(BF16)
    coarse = jnp.floor(key * (1.0 / 16.0)) * 16.0
    fine = (key - coarse).astype(BF16)
    coarse = coarse.astype(BF16)
    row, lane = iota((LANES, entries), 0), iota((LANES, entries), 1)
    own = ones_where(row == lane % LANES).astype(BF16)
    keyed = dot(fine, own) + dot(coarse, own)
    keyed = jnp.where(iota((STEP, entries), 0) == iota((STEP, entries), 1) // CAP, keyed, 0.0)
    key_row = jnp.sum(keyed, axis=0, keepdims=True).astype(I32)
    key_rows = gathered.shape[0]
    onehot = ones_where(iota((key_rows, entries), 0) == key_row).astype(BF16)
    slot = ones_where(iota((entries, STEP), 0) // CAP == iota((entries, STEP), 1)).astype(BF16)
    row, lane = iota((entries, LANES), 0), iota((entries, LANES), 1)
    own = lane == row % LANES
    every = jnp.ones((LANES, LANES), BF16)
    parts = [jnp.where(own, dot(slot, part), 0.0).astype(BF16) for part in (fine, coarse, group)]
    key = dot(parts[0], every) + dot(parts[1], every)
    group = dot(parts[2], every)
    here = pl.ds(pl.multiple_of(b * entries, entries), entries)
    keys[here, :] = key
    groups[here, :] = group
    blocks = recv[pl.ds(b * STEP, STEP)].reshape(entries, WIDTH)
    wide = 2 * LANES
    inside = (iota((entries, wide), 1) % LANES // NB).astype(F32) == jnp.concatenate([group, group], axis=1)
    for c in range(NB // 2):
        lanes = slice(c * wide, (c + 1) * wide)
        spaced = jnp.where(inside, dot(blocks, spread[:, lanes]), 0.0).astype(BF16)
        gathered[:, lanes] = gathered[:, lanes] + dot(onehot, spaced)


def pick(b, picked, keys, groups, fold, spaced, back):
    entries = STEP * CAP
    here = pl.ds(pl.multiple_of(b * entries, entries), entries)
    key, group = keys[here, :], groups[here, :]
    lane = iota((entries, LANES), 1).astype(F32)
    onehot = jnp.concatenate(
        [ones_where(lane + float(n * LANES) == key).astype(BF16) for n in range(picked.shape[0] // LANES)], axis=1
    )
    wide = 2 * LANES
    inside = (iota((entries, wide), 1) % LANES // NB).astype(F32) == jnp.concatenate([group, group], axis=1)
    for c in range(NB // 2):
        lanes = slice(c * wide, (c + 1) * wide)
        spaced[:, lanes] = jnp.where(inside, dot(onehot, picked[:, lanes]), 0.0).astype(BF16)
    blocks = dot(spaced[...], fold[...]).astype(BF16)
    back[pl.ds(b * STEP, STEP)] = blocks.reshape(STEP, CAP, WIDTH)


def potential_of(charge, below, above, left, right):
    rows = charge.shape[0]
    lane = iota((rows, LANES), 1)
    row = iota((rows, LANES), 0)
    swapped = pltpu.roll(charge, CY, 1)
    first_of_above = pltpu.roll(above, CY, 1)[0:1]
    last_of_below = pltpu.roll(below, CY, 1)[rows - 1 : rows]
    up = jnp.where(row == rows - 1, first_of_above, pltpu.roll(swapped, rows - 1, 0))
    next_x = jnp.where(lane < CY, swapped, up)
    down = jnp.where(row == 0, last_of_below, pltpu.roll(swapped, 1, 0))
    last_x = jnp.where(lane < CY, down, swapped)
    next_y = jnp.where(lane % CY == CY - 1, pltpu.roll(right, CY - 1, 1), pltpu.roll(charge, LANES - 1, 1))
    last_y = jnp.where(lane % CY == 0, pltpu.roll(left, LANES - CY + 1, 1), pltpu.roll(charge, 1, 1))
    slope_x = 0.5 * (next_x - last_x)
    slope_y = 0.5 * (next_y - last_y)
    return charge * lax.rsqrt(
        1.0 + charge * charge + gradient_weight * (slope_x * slope_x + slope_y * slope_y)
    )


def whole_kernel(
    tiles_hbm, slots_hbm, sizes_hbm, density_hbm, extent_hbm, basis_hbm, ones_hbm, spread_hbm, fold_hbm,
    out_hbm, potential_hbm,
    tiles_ref, slots_ref, sizes_ref, density_ref, extent_ref, ones_ref, spread_ref, fold_ref, out_ref, potential_ref,
    basis, weighted, chunks, recv, back, returned, codes, got, marks, picks, picks_turned, spread, fold, gathered, keys, groups,
    square, matrix, picked, spaced, charge, halo,
    send_sems, recv_sems, code_sems, return_sem, halo_send, halo_recv, local_sem,
):
    devices = chunks.shape[0]
    functions, cells = basis.shape
    atoms = functions // NB
    column_tiles = functions // LANES
    batches = devices // BATCH
    gx, gy = lax.axis_index("gx"), lax.axis_index("gy")
    load = pltpu.make_async_copy(basis_hbm, basis, local_sem.at[0])
    inputs = [
        pltpu.make_async_copy(source, target, local_sem.at[1 + n])
        for n, (source, target) in enumerate((
            (tiles_hbm, tiles_ref), (slots_hbm, slots_ref), (sizes_hbm, sizes_ref), (density_hbm, density_ref),
            (ones_hbm, ones_ref), (extent_hbm, extent_ref), (spread_hbm, spread_ref), (fold_hbm, fold_ref),
        ))
    ]
    for copy in inputs:
        copy.start()
    load.start()
    barrier = pltpu.get_barrier_semaphore()

    def greet(b, carry):
        for j, place in enumerate(places(b, gx, gy, True)):
            def signal():
                pl.semaphore_signal(barrier, inc=1, device_id=place, device_id_type=MESH)

            if j == 0:
                pl.when(b > 0)(signal)
            else:
                signal()
        return carry

    lax.fori_loop(0, batches, greet, 0)
    gathered[...] = jnp.zeros_like(gathered)
    for c in range(column_tiles):
        low, high = (c + 1) * LANES, (c // 3 + 1) * 3 * LANES
        if low < high:
            square[c, low:high, :] = jnp.zeros((high - low, LANES), F32)
        low, high = key_offset(c) + GROUPS * (c + 1), key_offset(c + 1)
        high = picked.shape[0] if c + 1 == column_tiles else high
        if low < high:
            picked[low:high, :] = jnp.zeros((high - low, picked.shape[1]), BF16)
    for copy in inputs[:5]:
        copy.wait()
    pairs = density_ref.shape[0]
    before, turned, eye = (ones_ref[:, n * WIDTH : (n + 1) * WIDTH].astype(BF16) for n in range(3))
    mask = size_mask_of(sizes_ref[...], eye)
    masked = jnp.where(mask, density_ref[...].astype(F32), 0.0).astype(BF16)
    blocks = jnp.concatenate([masked, dot(masked, turned).astype(BF16)], axis=0)
    asked = plan(tiles_ref[...], slots_ref, tile_of(iota((devices, 1), 0), gx, gy), before, marks)
    pl.semaphore_wait(barrier, devices - 1)
    rows_per_batch = BATCH * CAP // LANES

    def push(b, carry):
        for j, place in enumerate(places(b, gx, gy, True)):
            slot = b * BATCH + j
            row = b * rows_per_batch + j * CAP // LANES

            def start():
                remote(codes.at[row], got.at[slot], send_sems.at[0], code_sems.at[b], place).start()
                remote(chunks.at[slot], recv.at[slot], send_sems.at[1], recv_sems.at[b], place).start()

            def keep():
                pltpu.make_async_copy(codes.at[0], got.at[0], code_sems.at[0]).start()
                pltpu.make_async_copy(chunks.at[0], recv.at[0], recv_sems.at[0]).start()

            if j == 0:
                pl.when(b > 0)(start)
                pl.when(b == 0)(keep)
            else:
                start()
        return carry

    steps = devices // STEP
    per_step = STEP // BATCH

    def fill(n, carry):
        tile = tile_of(n * STEP + iota((1, STEP * CAP), 1) // CAP, gx, gy).astype(F32)
        pack(n, tile, asked, blocks, marks, chunks, codes, picks)
        return lax.fori_loop(n * per_step, (n + 1) * per_step, push, carry)

    lax.fori_loop(0, steps, fill, 0)
    for copy in inputs[5:]:
        copy.wait()
    spread[...] = spread_ref[...].astype(BF16)
    fold[...] = fold_ref[...].astype(BF16)
    load.wait()
    mask_basis(basis, extent_ref[...])

    def arrive(n, carry):
        for k in range(per_step):
            b = n * per_step + k
            slots = pl.ds(b * BATCH, BATCH)
            remote(got.at[slots], got.at[slots], send_sems.at[0], code_sems.at[b], (gx, gy)).wait_recv()
            remote(recv.at[slots], recv.at[slots], send_sems.at[1], recv_sems.at[b], (gx, gy)).wait_recv()
        collect(recv, got, n, spread, gathered, keys, groups)
        return carry

    lax.fori_loop(0, steps, arrive, 0)
    for c in range(column_tiles):
        low = key_offset(c)
        count = GROUPS * (c + 1)
        for i in range(NB):
            block = gathered[low : low + count, i * LANES : (i + 1) * LANES]
            square[c, pl.ds(i, count, stride=NB), :] = block
        matrix[:, c * LANES : (c + 1) * LANES] = square[c].astype(BF16)
    step = 2 * LANES
    part = 3 * LANES
    for c in range(cells // step):
        columns = basis[:, c * step : (c + 1) * step]
        total = jnp.zeros((1, step), F32)
        for low in range(0, functions, part):
            product = dot(matrix[low : low + part, low:], columns[low:])
            product = product * columns[low : low + part].astype(F32)
            total = total + jnp.sum(product, axis=0, keepdims=True)
        charge[2 * c : 2 * c + 1, :] = total[:, :LANES]
        charge[2 * c + 1 : 2 * c + 2, :] = total[:, LANES:]
    edges = [
        remote(charge, halo.at[n], halo_send.at[n], halo_recv.at[n], place)
        for n, place in enumerate(
            (((gx + 1) % 16, gy), ((gx + 15) % 16, gy), (gx, (gy + 7) % 8), (gx, (gy + 1) % 8))
        )
    ]
    for copy in edges:
        copy.start()
    for copy in edges:
        copy.wait()
    potential = potential_of(charge[...], halo[0], halo[1], halo[3], halo[2])
    for half in range(2):
        rows = potential if half == 0 else pltpu.roll(potential, CY, 1)
        potential_ref[pl.ds(half, CX // 2, stride=2), :] = rows[:, :CY]
    potential_out = pltpu.make_async_copy(potential_ref, potential_hbm, local_sem.at[1])
    potential_out.start()
    for c in range(cells // LANES):
        lanes = slice(c * LANES, (c + 1) * LANES)
        weighted[:, lanes] = (basis[:, lanes].astype(F32) * potential[c : c + 1]).astype(BF16)
    for start in range(0, column_tiles, 2):
        stop = min(start + 2, column_tiles)
        rows = weighted[start * LANES : stop * LANES, :]
        high = stop * LANES
        product = dot(basis[:high, :], rows, NT) * float(cells) ** -0.5
        for c in range(start, stop):
            square[c, :high, :] = product[:, (c - start) * LANES : (c - start + 1) * LANES]
            low = key_offset(c)
            count = GROUPS * (c + 1)
            for i in range(NB):
                block = square[c, pl.ds(i, count, stride=NB), :]
                picked[low : low + count, i * LANES : (i + 1) * LANES] = block.astype(BF16)
    keep = pltpu.make_async_copy(back.at[0], returned.at[0], return_sem)

    def hand_back(b, carry):
        for j, place in enumerate(places(b, gx, gy, False)):
            slot = b * BATCH + j

            def start():
                remote(back.at[slot], returned.at[slot], send_sems.at[2], return_sem, place).start()

            if j == 0:
                pl.when(b > 0)(start)
                pl.when(b == 0)(keep.start)
            else:
                start()
        return carry

    def give(n, carry):
        pick(n, picked, keys, groups, fold, spaced, back)
        return lax.fori_loop(n * per_step, (n + 1) * per_step, hand_back, carry)

    lax.fori_loop(0, steps, give, 0)
    for half in range(2):
        for n in range(devices * CAP // 512):
            part = picks[n * 512 : (n + 1) * 512, half * pairs : (half + 1) * pairs].astype(F32)
            lanes = half * devices * CAP + n * 512
            picks_turned[:, lanes : lanes + 512] = jnp.transpose(part).astype(BF16)
    mask = size_mask_of(sizes_ref[...], eye)
    remote(returned, returned, send_sems.at[2], return_sem, (gx, gy)).wait_recv()
    blocks = returned[...].reshape(devices * CAP, WIDTH)
    blocks = jnp.concatenate([blocks, dot(blocks, turned).astype(BF16)], axis=0)
    out_ref[...] = jnp.where(mask, dot(picks_turned[...], blocks), 0.0)
    out = pltpu.make_async_copy(out_ref, out_hbm, local_sem.at[2])
    out.start()
    out.wait()
    potential_out.wait()
    others = pl.ds(0, devices - 1)
    remote(got.at[others], got.at[others], send_sems.at[0], code_sems.at[0], (gx, gy)).wait_send()
    remote(chunks.at[others], recv.at[others], send_sems.at[1], recv_sems.at[0], (gx, gy)).wait_send()
    remote(back.at[others], returned.at[others], send_sems.at[2], return_sem, (gx, gy)).wait_send()


def finish_kernel(summed, field, out, potential):
    out[...] = summed[...]
    potential[...] = field[...]


VMEM_SPEC = pl.BlockSpec(memory_space=pltpu.VMEM)
ANY_SPEC = pl.BlockSpec(memory_space=pl.ANY)
DMA = pltpu.SemaphoreType.DMA


def shards(density, pair_tiles, pair_slots, pair_sizes, basis_table, tile_extent):
    devices = lax.axis_size("gx") * lax.axis_size("gy")
    pairs, targets = pair_tiles.shape
    atoms = tile_extent.shape[2]
    functions, cells = basis_table.shape[1:]
    rows = cells // LANES
    key_rows = key_offset(functions // LANES)
    chunk = pltpu.VMEM((devices, CAP, WIDTH), BF16)
    entries = devices * CAP
    spaced = NB * LANES
    results = pl.pallas_call(
        whole_kernel,
        name="whole",
        out_shape=[
            jax.ShapeDtypeStruct((pairs, WIDTH), F32),
            jax.ShapeDtypeStruct((CX, CY), F32),
        ],
        in_specs=[ANY_SPEC] * 9,
        out_specs=[ANY_SPEC] * 2,
        scratch_shapes=[
            pltpu.VMEM((targets, pairs), I32),
            pltpu.VMEM((targets, 2, pairs), I32),
            pltpu.VMEM((2, pairs), I32),
            pltpu.VMEM((pairs, WIDTH), BF16),
            pltpu.VMEM((2, atoms), I32),
            pltpu.VMEM((WIDTH, 3 * WIDTH), F32),
            pltpu.VMEM((WIDTH, spaced), F32),
            pltpu.VMEM((spaced, WIDTH), F32),
            pltpu.VMEM((pairs, WIDTH), F32),
            pltpu.VMEM((CX, CY), F32),
            pltpu.VMEM((functions, cells), BF16),
            pltpu.VMEM((functions, cells), BF16),
            chunk,
            chunk,
            chunk,
            chunk,
            pltpu.VMEM((devices * CAP // LANES, 1, LANES), F32),
            pltpu.VMEM((devices, 1, LANES), F32),
            pltpu.VMEM((devices, pairs), F32),
            pltpu.VMEM((entries, 2 * pairs), BF16),
            pltpu.VMEM((pairs, 2 * entries), BF16),
            pltpu.VMEM((WIDTH, spaced), BF16),
            pltpu.VMEM((spaced, WIDTH), BF16),
            pltpu.VMEM((key_rows, spaced), F32),
            pltpu.VMEM((entries, LANES), F32),
            pltpu.VMEM((entries, LANES), F32),
            pltpu.VMEM((functions // LANES, functions, LANES), F32),
            pltpu.VMEM((functions, functions), BF16),
            pltpu.VMEM((-(-key_rows // LANES) * LANES, spaced), BF16),
            pltpu.VMEM((STEP * CAP, spaced), BF16),
            pltpu.VMEM((rows, LANES), F32),
            pltpu.VMEM((4, rows, LANES), F32),
            DMA((3,)),
            DMA((devices // BATCH,)),
            DMA((devices // BATCH,)),
            DMA,
            DMA((4,)),
            DMA((4,)),
            DMA((9,)),
        ],
        compiler_params=pltpu.CompilerParams(
            vmem_limit_bytes=VMEM_BYTES, collective_id=1, has_side_effects=True
        ),
    )(pair_tiles.T, pair_slots.transpose(1, 2, 0), pair_sizes.T, density, tile_extent[0], basis_table[0], *constants())
    return tuple(pl.pallas_call(
        finish_kernel,
        name="finish",
        out_shape=[jax.ShapeDtypeStruct(result.shape, result.dtype) for result in results],
        in_specs=[VMEM_SPEC] * 2,
        out_specs=[VMEM_SPEC] * 2,
        compiler_params=pltpu.CompilerParams(vmem_limit_bytes=VMEM_BYTES),
    )(*results))


def solution(mesh):
    in_specs = (
        P(("gx", "gy"), None),
        P(("gx", "gy"), None),
        P(("gx", "gy"), None, None),
        P(("gx", "gy"), None),
        P(("gx", "gy"), None, None),
        P(("gx", "gy"), None, None),
    )
    out_specs = (P(("gx", "gy"), None), P("gx", "gy"))
    return jax.shard_map(shards, mesh=mesh, in_specs=in_specs, out_specs=out_specs, check_vma=False)
```

time: 74.3 us -> 66.9 us (0.900)
  Pallas kernels: 73.4 us -> 66.2 us
    pallas_call x1, Pallas kernels: 9.56 us -> 1.68 us  [shards(): pl.pallas_call(finish_kernel, name='finish', out_shape=[jax.ShapeDtypeStr...]
where the time goes in v2:
time: 66.9 us; the launch traced here: 66.8 us
  Pallas kernels  66.2 us (99%)
    pallas_call x1, Pallas kernels, shards(): pl.pallas_call(whole_kernel, name='whole', out_shape=[jax.ShapeDtypeStruc...  64.5 us
    pallas_call x1, Pallas kernels, shards(): pl.pallas_call(finish_kernel, name='finish', out_shape=[jax.ShapeDtypeStr...  1.68 us

profile of v2, /device:TPU:1, one launch (start us, length us, event | category | flops | bytes accessed | tf_op | source)
XLA Modules:
  0.0 66.8 jit_solution(16343360390506702561)
XLA Ops:
  0.6 64.5 %whole.1 = (f32[256,256]{1,0:T(8,128)}, f32[32,64]{1,0:T(8,128)}) custom-call(s32[4,256]{1,0:T(4,128)} %bitcast.7, s32[4,2,256]{2,1,0:T(2,128)} %bitcast.6, s32[2,256]{1,0:T(2,128)} %bitcast.8, bf16[256,256]{1,0:T(8,128)(2,1)} %density_hbm.1, s32[2,72]{1,0:T(2,128)} %bitcast.9, bf16[1152,2048]{1,0:T(8,128)(2,1)} %bitcast.5, ...), custom_call_target="tpu_custom_call" | custom-call | tf_op jit(solution)/shard_map/whole/pallas_call | solution.py:444
  65.1 1.7 %finish.1 = (f32[256,256]{1,0:T(8,128)}, f32[32,64]{1,0:T(8,128)}) custom-call(f32[256,256]{1,0:T(8,128)} %get-tuple-element.4.summed, f32[32,64]{1,0:T(8,128)} %get-tuple-element.5.field), custom_call_target="tpu_custom_call" | custom-call | tf_op jit(solution)/shard_map/finish/pallas_call | solution.py:498

commit v3 on v2

--- a/solution.py
+++ b/solution.py
@@ -72,24 +72,26 @@
     return jnp.concatenate(asked + [jnp.zeros((16 - 3 * targets, pairs), F32)], axis=0).astype(BF16)
 
 
-def pack(b, tile, asked, blocks, marks, chunks, codes, picks):
+def pack(n, blocks, marks, chunks, picks):
     pairs = marks.shape[1]
     entries = STEP * CAP
     own = (4 * (iota((entries, pairs), 0) % CAP)).astype(F32)
-    rows = jnp.broadcast_to(marks[pl.ds(b * STEP, STEP), :][:, None, :], (STEP, CAP, pairs))
+    rows = jnp.broadcast_to(marks[pl.ds(n * STEP, STEP), :][:, None, :], (STEP, CAP, pairs))
     rows = rows.reshape(entries, pairs) - own
     same, upper, lower = ones_where(rows == 0.0), ones_where(rows == 1.0), ones_where(rows == 2.0)
-    straight = (same + upper).astype(BF16)
-    across = lower.astype(BF16)
-    here = pl.ds(pl.multiple_of(b * entries, entries), entries)
-    picks[here, :pairs] = straight
-    picks[here, pairs:] = across
+    here = pl.ds(pl.multiple_of(n * entries, entries), entries)
+    picks[here, :pairs] = (same + upper).astype(BF16)
+    picks[here, pairs:] = lower.astype(BF16)
     weights = jnp.concatenate([(same + 2.0 * upper).astype(BF16), (2.0 * lower).astype(BF16)], axis=1)
-    chunks[pl.ds(b * STEP, STEP)] = dot(weights, blocks).astype(BF16).reshape(STEP, CAP, WIDTH)
-    told = dot(asked, straight + across, NT)
-    first = jnp.zeros((1, entries), F32)
-    second = jnp.zeros((1, entries), F32)
-    for k in range(asked.shape[0] // 3):
+    chunks[pl.ds(n * STEP, STEP)] = dot(weights, blocks).astype(BF16).reshape(STEP, CAP, WIDTH)
+
+
+def encode(asked, tile, picks, codes):
+    pairs = asked.shape[1]
+    told = dot(asked, picks[:, :pairs] + picks[:, pairs:], NT)
+    first = jnp.zeros(tile.shape, F32)
+    second = jnp.zeros(tile.shape, F32)
+    for k in range(asked.shape[0] // 4):
         hit = told[3 * k : 3 * k + 1] == tile
         first = first + jnp.where(hit, told[3 * k + 1 : 3 * k + 2], 0.0)
         second = second + jnp.where(hit, told[3 * k + 2 : 3 * k + 3], 0.0)
@@ -97,31 +99,37 @@
     half = jnp.floor(column_tile * 0.5)
     key = 16.0 * (half + 1.0) * (column_tile - half) + first
     code = key * GROUPS + (second - column_tile * GROUPS)
-    for n in range(entries // LANES):
-        codes[b * (entries // LANES) + n] = code[:, n * LANES : (n + 1) * LANES]
-
-
-INNER = [(j % 4, (j // 4 + j) % 4, (j + 3 * (j // 4)) % 4) for j in range(BATCH)]
-
-
-def places(b, gx, gy, outward):
+    for n in range(tile.shape[1] // LANES):
+        codes[n] = code[:, n * LANES : (n + 1) * LANES]
+
+
+INNER = [(j % 4, (j // 4 + j) % 4) for j in range(BATCH)]
+SHIFT = [(j + 3 * (j // 4)) % 4 for j in range(BATCH)]
+ROWS = BATCH * CAP // LANES
+
+
+def columns_of(batch):
+    return [(batch // 4) * 4 + (batch + SHIFT[j]) % 4 for j in range(BATCH)]
+
+
+def places(batch, gx, gy, outward):
     core = gy % 2
-    other = (core + b % 2) % 2
-    turn = 1 + 2 * core if outward else 3 - 2 * other
+    other = (core + batch // 4) % 2
+    turn = 1 + 2 * other if outward else 3 - 2 * core
     x, y, z = gx // 4, gx % 4, gy // 2
     xs = [((x + d * turn) % 4) * 4 for d in range(4)]
     ys = [(y + d * turn) % 4 for d in range(4)]
-    zs = [((z + (b // 2 + d) * turn) % 4) * 2 + other for d in range(4)]
-    return [(xs[dx] + ys[dy], zs[dz]) for dx, dy, dz in INNER]
+    zs = [((z + (batch + d) * turn) % 4) * 2 + other for d in range(4)]
+    return [(xs[dx] + ys[dy], zs[shift]) for (dx, dy), shift in zip(INNER, SHIFT)]
 
 
 def tile_of(slot, gx, gy):
     b, j = slot >> 4, slot & 15
-    dx, dy, dz = j & 3, ((j >> 2) + j) & 3, ((b >> 1) + j + 3 * (j >> 2)) & 3
-    core = gy % 2
-    turn = 1 + 2 * core
+    dx, dy, dz, dc = j & 3, ((j >> 2) + j) & 3, b & 3, b >> 2
+    other = (gy % 2 + dc) & 1
+    turn = 1 + 2 * other
     px = ((gx // 4 + dx * turn) & 3) * 4 + ((gx % 4 + dy * turn) & 3)
-    return px * 8 + ((gy // 2 + dz * turn) & 3) * 2 + ((core + b) & 1)
+    return px * 8 + ((gy // 2 + dz * turn) & 3) * 2 + other
 
 
 def remote(source, target, send_sem, recv_sem, place):
@@ -155,32 +163,26 @@
     return [np.asarray(x, np.float32) for x in (square, spread, spread.T)]
 
 
-def collect(recv, got, b, spread, gathered, keys, groups):
-    entries = STEP * CAP
-    codes = got[pl.ds(b * STEP, STEP), 0, :]
-    key = jnp.floor(codes * (1.0 / GROUPS))
-    group = (codes - key * GROUPS).astype(BF16)
-    coarse = jnp.floor(key * (1.0 / 16.0)) * 16.0
-    fine = (key - coarse).astype(BF16)
-    coarse = coarse.astype(BF16)
-    row, lane = iota((LANES, entries), 0), iota((LANES, entries), 1)
-    own = ones_where(row == lane % LANES).astype(BF16)
-    keyed = dot(fine, own) + dot(coarse, own)
-    keyed = jnp.where(iota((STEP, entries), 0) == iota((STEP, entries), 1) // CAP, keyed, 0.0)
-    key_row = jnp.sum(keyed, axis=0, keepdims=True).astype(I32)
+def collect(recv, got, n, spread, gathered, keys, groups):
+    entries = BATCH * CAP
+    own = iota((GROUPS, LANES), 0) == iota((GROUPS, LANES), 1) // CAP
+    held = got.shape[0] // BATCH
+    lines = [got[j * held + column * ROWS + j // GROUPS] for j, column in enumerate(columns_of(n))]
+    code = []
+    for h in range(ROWS):
+        part = jnp.concatenate(lines[h * GROUPS : (h + 1) * GROUPS], axis=0)
+        code.append(jnp.sum(jnp.where(own, part, 0.0), axis=0, keepdims=True))
+    code = jnp.concatenate(code, axis=1)
+    key_row = jnp.floor(code * (1.0 / GROUPS))
+    group_row = code - key_row * GROUPS
     key_rows = gathered.shape[0]
-    onehot = ones_where(iota((key_rows, entries), 0) == key_row).astype(BF16)
-    slot = ones_where(iota((entries, STEP), 0) // CAP == iota((entries, STEP), 1)).astype(BF16)
-    row, lane = iota((entries, LANES), 0), iota((entries, LANES), 1)
-    own = lane == row % LANES
-    every = jnp.ones((LANES, LANES), BF16)
-    parts = [jnp.where(own, dot(slot, part), 0.0).astype(BF16) for part in (fine, coarse, group)]
-    key = dot(parts[0], every) + dot(parts[1], every)
-    group = dot(parts[2], every)
-    here = pl.ds(pl.multiple_of(b * entries, entries), entries)
+    onehot = ones_where(iota((key_rows, entries), 0).astype(F32) == key_row).astype(BF16)
+    key = jnp.transpose(jnp.broadcast_to(key_row, (LANES, entries)))
+    group = jnp.transpose(jnp.broadcast_to(group_row, (LANES, entries)))
+    here = pl.ds(pl.multiple_of(n * entries, entries), entries)
     keys[here, :] = key
     groups[here, :] = group
-    blocks = recv[pl.ds(b * STEP, STEP)].reshape(entries, WIDTH)
+    blocks = recv[pl.ds(n * BATCH, BATCH)].reshape(entries, WIDTH)
     wide = 2 * LANES
     inside = (iota((entries, wide), 1) % LANES // NB).astype(F32) == jnp.concatenate([group, group], axis=1)
     for c in range(NB // 2):
@@ -190,7 +192,7 @@
 
 
 def pick(b, picked, keys, groups, fold, spaced, back):
-    entries = STEP * CAP
+    entries = BATCH * CAP
     here = pl.ds(pl.multiple_of(b * entries, entries), entries)
     key, group = keys[here, :], groups[here, :]
     lane = iota((entries, LANES), 1).astype(F32)
@@ -203,7 +205,7 @@
         lanes = slice(c * wide, (c + 1) * wide)
         spaced[:, lanes] = jnp.where(inside, dot(onehot, picked[:, lanes]), 0.0).astype(BF16)
     blocks = dot(spaced[...], fold[...]).astype(BF16)
-    back[pl.ds(b * STEP, STEP)] = blocks.reshape(STEP, CAP, WIDTH)
+    back[pl.ds(b * BATCH, BATCH)] = blocks.reshape(BATCH, CAP, WIDTH)
 
 
 def potential_of(charge, below, above, left, right):
@@ -230,9 +232,9 @@
     tiles_hbm, slots_hbm, sizes_hbm, density_hbm, extent_hbm, basis_hbm, ones_hbm, spread_hbm, fold_hbm,
     out_hbm, potential_hbm,
     tiles_ref, slots_ref, sizes_ref, density_ref, extent_ref, ones_ref, spread_ref, fold_ref, out_ref, potential_ref,
-    basis, weighted, chunks, recv, back, returned, codes, got, marks, picks, picks_turned, spread, fold, gathered, keys, groups,
+    basis, weighted, chunks, recv, back, returned, codes, handed, got, marks, picks, picks_turned, spread, fold, gathered, keys, groups,
     square, matrix, picked, spaced, charge, halo,
-    send_sems, recv_sems, code_sems, return_sem, halo_send, halo_recv, local_sem,
+    send_sems, recv_sems, hand_sem, code_sem, return_sem, halo_send, halo_recv, local_sem,
 ):
     devices = chunks.shape[0]
     functions, cells = basis.shape
@@ -267,8 +269,8 @@
     lax.fori_loop(0, batches, greet, 0)
     gathered[...] = jnp.zeros_like(gathered)
     for c in range(column_tiles):
-        low, high = (c + 1) * LANES, (c // 3 + 1) * 3 * LANES
-        if low < high:
+        low, high = (c + 1) * LANES, (c + 2) * LANES
+        if c % 2 == 1:
             square[c, low:high, :] = jnp.zeros((high - low, LANES), F32)
         low, high = key_offset(c) + GROUPS * (c + 1), key_offset(c + 1)
         high = picked.shape[0] if c + 1 == column_tiles else high
@@ -283,54 +285,68 @@
     blocks = jnp.concatenate([masked, dot(masked, turned).astype(BF16)], axis=0)
     asked = plan(tiles_ref[...], slots_ref, tile_of(iota((devices, 1), 0), gx, gy), before, marks)
     pl.semaphore_wait(barrier, devices - 1)
-    rows_per_batch = BATCH * CAP // LANES
-
-    def push(b, carry):
-        for j, place in enumerate(places(b, gx, gy, True)):
-            slot = b * BATCH + j
-            row = b * rows_per_batch + j * CAP // LANES
+    steps = devices // STEP
+
+    def push(batch, carry):
+        for j, (column, place) in enumerate(zip(columns_of(batch), places(batch, gx, gy, True))):
+            slot, spot = column * BATCH + j, batch * BATCH + j
 
             def start():
-                remote(codes.at[row], got.at[slot], send_sems.at[0], code_sems.at[b], place).start()
-                remote(chunks.at[slot], recv.at[slot], send_sems.at[1], recv_sems.at[b], place).start()
+                remote(chunks.at[slot], recv.at[spot], send_sems.at[1], recv_sems.at[batch], place).start()
 
             def keep():
-                pltpu.make_async_copy(codes.at[0], got.at[0], code_sems.at[0]).start()
                 pltpu.make_async_copy(chunks.at[0], recv.at[0], recv_sems.at[0]).start()
 
             if j == 0:
-                pl.when(b > 0)(start)
-                pl.when(b == 0)(keep)
+                pl.when(batch > 0)(start)
+                pl.when(batch == 0)(keep)
             else:
                 start()
         return carry
 
-    steps = devices // STEP
-    per_step = STEP // BATCH
-
     def fill(n, carry):
-        tile = tile_of(n * STEP + iota((1, STEP * CAP), 1) // CAP, gx, gy).astype(F32)
-        pack(n, tile, asked, blocks, marks, chunks, codes, picks)
-        return lax.fori_loop(n * per_step, (n + 1) * per_step, push, carry)
-
-    lax.fori_loop(0, steps, fill, 0)
+        pack(n, blocks, marks, chunks, picks)
+        return carry
+
+    early = 2
+    lax.fori_loop(0, steps // 2, fill, 0)
+    lax.fori_loop(0, early, push, 0)
+    lax.fori_loop(steps // 2, steps, fill, 0)
+    tile = tile_of(iota((1, devices * CAP), 1) // CAP, gx, gy).astype(F32)
+    encode(asked, tile, picks, codes)
+    pltpu.make_async_copy(codes.at[pl.ds(0, ROWS)], handed.at[pl.ds(0, ROWS)], hand_sem).start()
+    for column in range(1, batches):
+        rows = pl.ds(column * ROWS, ROWS)
+        dc = column // 4
+        other = (gy % 2 + dc) % 2
+        place = (gx, ((gy // 2 + column % 4 * (1 + 2 * other)) % 4) * 2 + other)
+        remote(codes.at[rows], handed.at[rows], send_sems.at[0], hand_sem, place).start()
     for copy in inputs[5:]:
         copy.wait()
     spread[...] = spread_ref[...].astype(BF16)
     fold[...] = fold_ref[...].astype(BF16)
     load.wait()
     mask_basis(basis, extent_ref[...])
+    held = handed.shape[0]
+    remote(handed, handed, send_sems.at[0], hand_sem, (gx, gy)).wait_recv()
+    pltpu.make_async_copy(handed, got.at[pl.ds(0, held)], code_sem).start()
+    along = [
+        (((gx // 4 + dx * (1 + 2 * (gy % 2))) % 4) * 4 + (gx % 4 + dy * (1 + 2 * (gy % 2))) % 4, gy)
+        for dx, dy in INNER
+    ]
+    for j in range(1, BATCH):
+        remote(handed, got.at[pl.ds(j * held, held)], send_sems.at[0], code_sem, along[j]).start()
+    lax.fori_loop(early, batches, push, 0)
+
+    remote(got, got, send_sems.at[0], code_sem, (gx, gy)).wait_recv()
 
     def arrive(n, carry):
-        for k in range(per_step):
-            b = n * per_step + k
-            slots = pl.ds(b * BATCH, BATCH)
-            remote(got.at[slots], got.at[slots], send_sems.at[0], code_sems.at[b], (gx, gy)).wait_recv()
-            remote(recv.at[slots], recv.at[slots], send_sems.at[1], recv_sems.at[b], (gx, gy)).wait_recv()
+        slots = pl.ds(n * BATCH, BATCH)
+        remote(recv.at[slots], recv.at[slots], send_sems.at[1], recv_sems.at[n], (gx, gy)).wait_recv()
         collect(recv, got, n, spread, gathered, keys, groups)
         return carry
 
-    lax.fori_loop(0, steps, arrive, 0)
+    lax.fori_loop(0, batches, arrive, 0)
     for c in range(column_tiles):
         low = key_offset(c)
         count = GROUPS * (c + 1)
@@ -339,13 +355,13 @@
             square[c, pl.ds(i, count, stride=NB), :] = block
         matrix[:, c * LANES : (c + 1) * LANES] = square[c].astype(BF16)
     step = 2 * LANES
-    part = 3 * LANES
+    cuts = [0] + list(range(LANES, functions + 1, 2 * LANES))
     for c in range(cells // step):
         columns = basis[:, c * step : (c + 1) * step]
         total = jnp.zeros((1, step), F32)
-        for low in range(0, functions, part):
-            product = dot(matrix[low : low + part, low:], columns[low:])
-            product = product * columns[low : low + part].astype(F32)
+        for low, high in zip(cuts, cuts[1:]):
+            product = dot(matrix[low:high, low:], columns[low:])
+            product = product * columns[low:high].astype(F32)
             total = total + jnp.sum(product, axis=0, keepdims=True)
         charge[2 * c : 2 * c + 1, :] = total[:, :LANES]
         charge[2 * c + 1 : 2 * c + 2, :] = total[:, LANES:]
@@ -368,13 +384,10 @@
     for c in range(cells // LANES):
         lanes = slice(c * LANES, (c + 1) * LANES)
         weighted[:, lanes] = (basis[:, lanes].astype(F32) * potential[c : c + 1]).astype(BF16)
-    for start in range(0, column_tiles, 2):
-        stop = min(start + 2, column_tiles)
-        rows = weighted[start * LANES : stop * LANES, :]
-        high = stop * LANES
-        product = dot(basis[:high, :], rows, NT) * float(cells) ** -0.5
-        for c in range(start, stop):
-            square[c, :high, :] = product[:, (c - start) * LANES : (c - start + 1) * LANES]
+    for start, high in zip(cuts, cuts[1:]):
+        product = dot(basis[:high, :], weighted[start:high, :], NT)
+        for c in range(start // LANES, high // LANES):
+            square[c, :high, :] = product[:, c * LANES - start : (c + 1) * LANES - start]
             low = key_offset(c)
             count = GROUPS * (c + 1)
             for i in range(NB):
@@ -382,25 +395,22 @@
                 picked[low : low + count, i * LANES : (i + 1) * LANES] = block.astype(BF16)
     keep = pltpu.make_async_copy(back.at[0], returned.at[0], return_sem)
 
-    def hand_back(b, carry):
-        for j, place in enumerate(places(b, gx, gy, False)):
-            slot = b * BATCH + j
+    def give(n, carry):
+        pick(n, picked, keys, groups, fold, spaced, back)
+        for j, (column, place) in enumerate(zip(columns_of(n), places(n, gx, gy, False))):
+            slot, spot = column * BATCH + j, n * BATCH + j
 
             def start():
-                remote(back.at[slot], returned.at[slot], send_sems.at[2], return_sem, place).start()
+                remote(back.at[spot], returned.at[slot], send_sems.at[2], return_sem, place).start()
 
             if j == 0:
-                pl.when(b > 0)(start)
-                pl.when(b == 0)(keep.start)
+                pl.when(n > 0)(start)
+                pl.when(n == 0)(keep.start)
             else:
                 start()
         return carry
 
-    def give(n, carry):
-        pick(n, picked, keys, groups, fold, spaced, back)
-        return lax.fori_loop(n * per_step, (n + 1) * per_step, hand_back, carry)
-
-    lax.fori_loop(0, steps, give, 0)
+    lax.fori_loop(0, batches, give, 0)
     for half in range(2):
         for n in range(devices * CAP // 512):
             part = picks[n * 512 : (n + 1) * 512, half * pairs : (half + 1) * pairs].astype(F32)
@@ -410,13 +420,16 @@
     remote(returned, returned, send_sems.at[2], return_sem, (gx, gy)).wait_recv()
     blocks = returned[...].reshape(devices * CAP, WIDTH)
     blocks = jnp.concatenate([blocks, dot(blocks, turned).astype(BF16)], axis=0)
-    out_ref[...] = jnp.where(mask, dot(picks_turned[...], blocks), 0.0)
+    out_ref[...] = jnp.where(mask, dot(picks_turned[...], blocks) * float(cells) ** -0.5, 0.0)
     out = pltpu.make_async_copy(out_ref, out_hbm, local_sem.at[2])
     out.start()
     out.wait()
     potential_out.wait()
     others = pl.ds(0, devices - 1)
-    remote(got.at[others], got.at[others], send_sems.at[0], code_sems.at[0], (gx, gy)).wait_send()
+    rows = pl.ds(ROWS, held - ROWS)
+    remote(handed.at[rows], handed.at[rows], send_sems.at[0], hand_sem, (gx, gy)).wait_send()
+    rows = pl.ds(held, got.shape[0] - held)
+    remote(got.at[rows], got.at[rows], send_sems.at[0], code_sem, (gx, gy)).wait_send()
     remote(chunks.at[others], recv.at[others], send_sems.at[1], recv_sems.at[0], (gx, gy)).wait_send()
     remote(back.at[others], returned.at[others], send_sems.at[2], return_sem, (gx, gy)).wait_send()
 
@@ -468,7 +481,8 @@
             chunk,
             chunk,
             pltpu.VMEM((devices * CAP // LANES, 1, LANES), F32),
-            pltpu.VMEM((devices, 1, LANES), F32),
+            pltpu.VMEM((devices * CAP // LANES, 1, LANES), F32),
+            pltpu.VMEM((devices * CAP // LANES * BATCH, 1, LANES), F32),
             pltpu.VMEM((devices, pairs), F32),
             pltpu.VMEM((entries, 2 * pairs), BF16),
             pltpu.VMEM((pairs, 2 * entries), BF16),
@@ -480,12 +494,13 @@
             pltpu.VMEM((functions // LANES, functions, LANES), F32),
             pltpu.VMEM((functions, functions), BF16),
             pltpu.VMEM((-(-key_rows // LANES) * LANES, spaced), BF16),
-            pltpu.VMEM((STEP * CAP, spaced), BF16),
+            pltpu.VMEM((BATCH * CAP, spaced), BF16),
             pltpu.VMEM((rows, LANES), F32),
             pltpu.VMEM((4, rows, LANES), F32),
             DMA((3,)),
             DMA((devices // BATCH,)),
-            DMA((devices // BATCH,)),
+            DMA,
+            DMA,
             DMA,
             DMA((4,)),
             DMA((4,)),

time: 66.9 us -> 69.5 us (1.039)
  Pallas kernels: 66.2 us -> 68.8 us
    pallas_call x1, Pallas kernels: 64.5 us -> 67.1 us  [shards(): pl.pallas_call(whole_kernel, name='whole', out_shape=[jax.ShapeDtypeStruc...]
where the time goes in v3:
time: 69.5 us; the launch traced here: 69.4 us
  Pallas kernels  68.8 us (99%)
    pallas_call x1, Pallas kernels, shards(): pl.pallas_call(whole_kernel, name='whole', out_shape=[jax.ShapeDtypeStruc...  67.1 us
    pallas_call x1, Pallas kernels, shards(): pl.pallas_call(finish_kernel, name='finish', out_shape=[jax.ShapeDtypeStr...  1.68 us

profile of v3, /device:TPU:1, one launch (start us, length us, event | category | flops | bytes accessed | tf_op | source)
XLA Modules:
  0.0 69.4 jit_solution(8112425894771973058)
XLA Ops:
  0.6 67.1 %whole.1 = (f32[256,256]{1,0:T(8,128)}, f32[32,64]{1,0:T(8,128)}) custom-call(s32[4,256]{1,0:T(4,128)} %bitcast.7, s32[4,2,256]{2,1,0:T(2,128)} %bitcast.6, s32[2,256]{1,0:T(2,128)} %bitcast.8, bf16[256,256]{1,0:T(8,128)(2,1)} %density_hbm.1, s32[2,72]{1,0:T(2,128)} %bitcast.9, bf16[1152,2048]{1,0:T(8,128)(2,1)} %bitcast.5, ...), custom_call_target="tpu_custom_call" | custom-call | tf_op jit(solution)/shard_map/whole/pallas_call | solution.py:457
  67.7 1.7 %finish.1 = (f32[256,256]{1,0:T(8,128)}, f32[32,64]{1,0:T(8,128)}) custom-call(f32[256,256]{1,0:T(8,128)} %get-tuple-element.4.summed, f32[32,64]{1,0:T(8,128)} %get-tuple-element.5.field), custom_call_target="tpu_custom_call" | custom-call | tf_op jit(solution)/shard_map/finish/pallas_call | solution.py:513

commit v4 on v2

--- a/solution.py
+++ b/solution.py
@@ -156,31 +156,23 @@
 
 
 def collect(recv, got, b, spread, gathered, keys, groups):
-    entries = STEP * CAP
-    codes = got[pl.ds(b * STEP, STEP), 0, :]
-    key = jnp.floor(codes * (1.0 / GROUPS))
-    group = (codes - key * GROUPS).astype(BF16)
-    coarse = jnp.floor(key * (1.0 / 16.0)) * 16.0
-    fine = (key - coarse).astype(BF16)
-    coarse = coarse.astype(BF16)
-    row, lane = iota((LANES, entries), 0), iota((LANES, entries), 1)
-    own = ones_where(row == lane % LANES).astype(BF16)
-    keyed = dot(fine, own) + dot(coarse, own)
-    keyed = jnp.where(iota((STEP, entries), 0) == iota((STEP, entries), 1) // CAP, keyed, 0.0)
-    key_row = jnp.sum(keyed, axis=0, keepdims=True).astype(I32)
+    entries = BATCH * CAP
+    own = iota((GROUPS, LANES), 0) == iota((GROUPS, LANES), 1) // CAP
+    code = []
+    for h in range(BATCH // GROUPS):
+        lines = got[pl.ds(b * BATCH + h * GROUPS, GROUPS), 0, :]
+        code.append(jnp.sum(jnp.where(own, lines, 0.0), axis=0, keepdims=True))
+    code = jnp.concatenate(code, axis=1)
+    key_row = jnp.floor(code * (1.0 / GROUPS))
+    group_row = code - key_row * GROUPS
     key_rows = gathered.shape[0]
-    onehot = ones_where(iota((key_rows, entries), 0) == key_row).astype(BF16)
-    slot = ones_where(iota((entries, STEP), 0) // CAP == iota((entries, STEP), 1)).astype(BF16)
-    row, lane = iota((entries, LANES), 0), iota((entries, LANES), 1)
-    own = lane == row % LANES
-    every = jnp.ones((LANES, LANES), BF16)
-    parts = [jnp.where(own, dot(slot, part), 0.0).astype(BF16) for part in (fine, coarse, group)]
-    key = dot(parts[0], every) + dot(parts[1], every)
-    group = dot(parts[2], every)
+    onehot = ones_where(iota((key_rows, entries), 0).astype(F32) == key_row).astype(BF16)
+    key = jnp.transpose(jnp.broadcast_to(key_row, (LANES, entries)))
+    group = jnp.transpose(jnp.broadcast_to(group_row, (LANES, entries)))
     here = pl.ds(pl.multiple_of(b * entries, entries), entries)
     keys[here, :] = key
     groups[here, :] = group
-    blocks = recv[pl.ds(b * STEP, STEP)].reshape(entries, WIDTH)
+    blocks = recv[pl.ds(b * BATCH, BATCH)].reshape(entries, WIDTH)
     wide = 2 * LANES
     inside = (iota((entries, wide), 1) % LANES // NB).astype(F32) == jnp.concatenate([group, group], axis=1)
     for c in range(NB // 2):
@@ -190,7 +182,7 @@
 
 
 def pick(b, picked, keys, groups, fold, spaced, back):
-    entries = STEP * CAP
+    entries = BATCH * CAP
     here = pl.ds(pl.multiple_of(b * entries, entries), entries)
     key, group = keys[here, :], groups[here, :]
     lane = iota((entries, LANES), 1).astype(F32)
@@ -203,7 +195,7 @@
         lanes = slice(c * wide, (c + 1) * wide)
         spaced[:, lanes] = jnp.where(inside, dot(onehot, picked[:, lanes]), 0.0).astype(BF16)
     blocks = dot(spaced[...], fold[...]).astype(BF16)
-    back[pl.ds(b * STEP, STEP)] = blocks.reshape(STEP, CAP, WIDTH)
+    back[pl.ds(b * BATCH, BATCH)] = blocks.reshape(BATCH, CAP, WIDTH)
 
 
 def potential_of(charge, below, above, left, right):
@@ -282,7 +274,6 @@
     masked = jnp.where(mask, density_ref[...].astype(F32), 0.0).astype(BF16)
     blocks = jnp.concatenate([masked, dot(masked, turned).astype(BF16)], axis=0)
     asked = plan(tiles_ref[...], slots_ref, tile_of(iota((devices, 1), 0), gx, gy), before, marks)
-    pl.semaphore_wait(barrier, devices - 1)
     rows_per_batch = BATCH * CAP // LANES
 
     def push(b, carry):
@@ -305,15 +296,14 @@
                 start()
         return carry
 
-    steps = devices // STEP
-    per_step = STEP // BATCH
-
     def fill(n, carry):
         tile = tile_of(n * STEP + iota((1, STEP * CAP), 1) // CAP, gx, gy).astype(F32)
         pack(n, tile, asked, blocks, marks, chunks, codes, picks)
-        return lax.fori_loop(n * per_step, (n + 1) * per_step, push, carry)
-
-    lax.fori_loop(0, steps, fill, 0)
+        return carry
+
+    lax.fori_loop(0, devices // STEP, fill, 0)
+    pl.semaphore_wait(barrier, devices - 1)
+    lax.fori_loop(0, batches, push, 0)
     for copy in inputs[5:]:
         copy.wait()
     spread[...] = spread_ref[...].astype(BF16)
@@ -321,16 +311,14 @@
     load.wait()
     mask_basis(basis, extent_ref[...])
 
-    def arrive(n, carry):
-        for k in range(per_step):
-            b = n * per_step + k
-            slots = pl.ds(b * BATCH, BATCH)
-            remote(got.at[slots], got.at[slots], send_sems.at[0], code_sems.at[b], (gx, gy)).wait_recv()
-            remote(recv.at[slots], recv.at[slots], send_sems.at[1], recv_sems.at[b], (gx, gy)).wait_recv()
-        collect(recv, got, n, spread, gathered, keys, groups)
+    def arrive(b, carry):
+        slots = pl.ds(b * BATCH, BATCH)
+        remote(got.at[slots], got.at[slots], send_sems.at[0], code_sems.at[b], (gx, gy)).wait_recv()
+        remote(recv.at[slots], recv.at[slots], send_sems.at[1], recv_sems.at[b], (gx, gy)).wait_recv()
+        collect(recv, got, b, spread, gathered, keys, groups)
         return carry
 
-    lax.fori_loop(0, steps, arrive, 0)
+    lax.fori_loop(0, batches, arrive, 0)
     for c in range(column_tiles):
         low = key_offset(c)
         count = GROUPS * (c + 1)
@@ -372,7 +360,7 @@
         stop = min(start + 2, column_tiles)
         rows = weighted[start * LANES : stop * LANES, :]
         high = stop * LANES
-        product = dot(basis[:high, :], rows, NT) * float(cells) ** -0.5
+        product = dot(basis[:high, :], rows, NT)
         for c in range(start, stop):
             square[c, :high, :] = product[:, (c - start) * LANES : (c - start + 1) * LANES]
             low = key_offset(c)
@@ -382,7 +370,8 @@
                 picked[low : low + count, i * LANES : (i + 1) * LANES] = block.astype(BF16)
     keep = pltpu.make_async_copy(back.at[0], returned.at[0], return_sem)
 
-    def hand_back(b, carry):
+    def give(b, carry):
+        pick(b, picked, keys, groups, fold, spaced, back)
         for j, place in enumerate(places(b, gx, gy, False)):
             slot = b * BATCH + j
 
@@ -396,11 +385,7 @@
                 start()
         return carry
 
-    def give(n, carry):
-        pick(n, picked, keys, groups, fold, spaced, back)
-        return lax.fori_loop(n * per_step, (n + 1) * per_step, hand_back, carry)
-
-    lax.fori_loop(0, steps, give, 0)
+    lax.fori_loop(0, batches, give, 0)
     for half in range(2):
         for n in range(devices * CAP // 512):
             part = picks[n * 512 : (n + 1) * 512, half * pairs : (half + 1) * pairs].astype(F32)
@@ -410,7 +395,7 @@
     remote(returned, returned, send_sems.at[2], return_sem, (gx, gy)).wait_recv()
     blocks = returned[...].reshape(devices * CAP, WIDTH)
     blocks = jnp.concatenate([blocks, dot(blocks, turned).astype(BF16)], axis=0)
-    out_ref[...] = jnp.where(mask, dot(picks_turned[...], blocks), 0.0)
+    out_ref[...] = jnp.where(mask, dot(picks_turned[...], blocks) * float(cells) ** -0.5, 0.0)
     out = pltpu.make_async_copy(out_ref, out_hbm, local_sem.at[2])
     out.start()
     out.wait()
@@ -480,7 +465,7 @@
             pltpu.VMEM((functions // LANES, functions, LANES), F32),
             pltpu.VMEM((functions, functions), BF16),
             pltpu.VMEM((-(-key_rows // LANES) * LANES, spaced), BF16),
-            pltpu.VMEM((STEP * CAP, spaced), BF16),
+            pltpu.VMEM((BATCH * CAP, spaced), BF16),
             pltpu.VMEM((rows, LANES), F32),
             pltpu.VMEM((4, rows, LANES), F32),
             DMA((3,)),

time: 66.9 us -> 65.7 us (0.982)
  Pallas kernels: 66.2 us -> 64.9 us
    pallas_call x1, Pallas kernels: 64.5 us -> 63.2 us  [shards(): pl.pallas_call(whole_kernel, name='whole', out_shape=[jax.ShapeDtypeStruc...]
where the time goes in v4:
time: 65.7 us; the launch traced here: 65.5 us
  Pallas kernels  64.9 us (99%)
    pallas_call x1, Pallas kernels, shards(): pl.pallas_call(whole_kernel, name='whole', out_shape=[jax.ShapeDtypeStruc...  63.2 us
    pallas_call x1, Pallas kernels, shards(): pl.pallas_call(finish_kernel, name='finish', out_shape=[jax.ShapeDtypeStr...  1.68 us

profile of v4, /device:TPU:1, one launch (start us, length us, event | category | flops | bytes accessed | tf_op | source)
XLA Modules:
  0.0 65.5 jit_solution(8670785065053512664)
XLA Ops:
  0.6 63.2 %whole.1 = (f32[256,256]{1,0:T(8,128)}, f32[32,64]{1,0:T(8,128)}) custom-call(s32[4,256]{1,0:T(4,128)} %bitcast.7, s32[4,2,256]{2,1,0:T(2,128)} %bitcast.6, s32[2,256]{1,0:T(2,128)} %bitcast.8, bf16[256,256]{1,0:T(8,128)(2,1)} %density_hbm.1, s32[2,72]{1,0:T(2,128)} %bitcast.9, bf16[1152,2048]{1,0:T(8,128)(2,1)} %bitcast.5, ...), custom_call_target="tpu_custom_call" | custom-call | tf_op jit(solution)/shard_map/whole/pallas_call | solution.py:429
  63.9 1.7 %finish.1 = (f32[256,256]{1,0:T(8,128)}, f32[32,64]{1,0:T(8,128)}) custom-call(f32[256,256]{1,0:T(8,128)} %get-tuple-element.4.summed, f32[32,64]{1,0:T(8,128)} %get-tuple-element.5.field), custom_call_target="tpu_custom_call" | custom-call | tf_op jit(solution)/shard_map/finish/pallas_call | solution.py:483

commit v5 on v4

--- a/solution.py
+++ b/solution.py
@@ -79,8 +79,8 @@
     rows = jnp.broadcast_to(marks[pl.ds(b * STEP, STEP), :][:, None, :], (STEP, CAP, pairs))
     rows = rows.reshape(entries, pairs) - own
     same, upper, lower = ones_where(rows == 0.0), ones_where(rows == 1.0), ones_where(rows == 2.0)
-    straight = (same + upper).astype(BF16)
-    across = lower.astype(BF16)
+    straight = upper.astype(BF16)
+    across = (same + lower).astype(BF16)
     here = pl.ds(pl.multiple_of(b * entries, entries), entries)
     picks[here, :pairs] = straight
     picks[here, pairs:] = across
@@ -222,7 +222,7 @@
     tiles_hbm, slots_hbm, sizes_hbm, density_hbm, extent_hbm, basis_hbm, ones_hbm, spread_hbm, fold_hbm,
     out_hbm, potential_hbm,
     tiles_ref, slots_ref, sizes_ref, density_ref, extent_ref, ones_ref, spread_ref, fold_ref, out_ref, potential_ref,
-    basis, weighted, chunks, recv, back, returned, codes, got, marks, picks, picks_turned, spread, fold, gathered, keys, groups,
+    basis, weighted, upright, chunks, recv, back, returned, codes, got, marks, picks, picks_turned, spread, fold, gathered, keys, groups,
     square, matrix, picked, spaced, charge, halo,
     send_sems, recv_sems, code_sems, return_sem, halo_send, halo_recv, local_sem,
 ):
@@ -310,6 +310,9 @@
     fold[...] = fold_ref[...].astype(BF16)
     load.wait()
     mask_basis(basis, extent_ref[...])
+    for c in range(column_tiles):
+        lanes = slice(c * LANES, (c + 1) * LANES)
+        upright[:, lanes] = jnp.transpose(basis[lanes, :].astype(F32)).astype(BF16)
 
     def arrive(b, carry):
         slots = pl.ds(b * BATCH, BATCH)
@@ -358,9 +361,8 @@
         weighted[:, lanes] = (basis[:, lanes].astype(F32) * potential[c : c + 1]).astype(BF16)
     for start in range(0, column_tiles, 2):
         stop = min(start + 2, column_tiles)
-        rows = weighted[start * LANES : stop * LANES, :]
         high = stop * LANES
-        product = dot(basis[:high, :], rows, NT)
+        product = dot(weighted[:high, :], upright[:, start * LANES : high])
         for c in range(start, stop):
             square[c, :high, :] = product[:, (c - start) * LANES : (c - start + 1) * LANES]
             low = key_offset(c)
@@ -448,6 +450,7 @@
             pltpu.VMEM((CX, CY), F32),
             pltpu.VMEM((functions, cells), BF16),
             pltpu.VMEM((functions, cells), BF16),
+            pltpu.VMEM((cells, functions), BF16),
             chunk,
             chunk,
             chunk,

time: 65.7 us -> 65.5 us (level)
  no operation moved by 1% of the time
where the time goes in v5:
time: 65.5 us; the launch traced here: 65.3 us
  Pallas kernels  64.7 us (99%)
    pallas_call x1, Pallas kernels, shards(): pl.pallas_call(whole_kernel, name='whole', out_shape=[jax.ShapeDtypeStruc...  63 us
    pallas_call x1, Pallas kernels, shards(): pl.pallas_call(finish_kernel, name='finish', out_shape=[jax.ShapeDtypeStr...  1.68 us

profile of v5, /device:TPU:1, one launch (start us, length us, event | category | flops | bytes accessed | tf_op | source)
XLA Modules:
  0.0 65.3 jit_solution(6152703943715568438)
XLA Ops:
  0.6 63.0 %whole.1 = (f32[256,256]{1,0:T(8,128)}, f32[32,64]{1,0:T(8,128)}) custom-call(s32[4,256]{1,0:T(4,128)} %bitcast.7, s32[4,2,256]{2,1,0:T(2,128)} %bitcast.6, s32[2,256]{1,0:T(2,128)} %bitcast.8, bf16[256,256]{1,0:T(8,128)(2,1)} %density_hbm.1, s32[2,72]{1,0:T(2,128)} %bitcast.9, bf16[1152,2048]{1,0:T(8,128)(2,1)} %bitcast.5, ...), custom_call_target="tpu_custom_call" | custom-call | tf_op jit(solution)/shard_map/whole/pallas_call | solution.py:431
  63.6 1.7 %finish.1 = (f32[256,256]{1,0:T(8,128)}, f32[32,64]{1,0:T(8,128)}) custom-call(f32[256,256]{1,0:T(8,128)} %get-tuple-element.4.summed, f32[32,64]{1,0:T(8,128)} %get-tuple-element.5.field), custom_call_target="tpu_custom_call" | custom-call | tf_op jit(solution)/shard_map/finish/pallas_call | solution.py:486

commit v6 on v5

--- a/solution.py
+++ b/solution.py
@@ -34,6 +34,10 @@
     return lax.dot_general(a, b, dims, preferred_element_type=F32)
 
 
+def span(n, size):
+    return pl.ds(n * size if isinstance(n, int) else pl.multiple_of(n * size, size), size)
+
+
 def ones_where(condition):
     return jnp.where(condition, 1.0, 0.0)
 
@@ -81,7 +85,7 @@
     same, upper, lower = ones_where(rows == 0.0), ones_where(rows == 1.0), ones_where(rows == 2.0)
     straight = upper.astype(BF16)
     across = (same + lower).astype(BF16)
-    here = pl.ds(pl.multiple_of(b * entries, entries), entries)
+    here = span(b, entries)
     picks[here, :pairs] = straight
     picks[here, pairs:] = across
     weights = jnp.concatenate([(same + 2.0 * upper).astype(BF16), (2.0 * lower).astype(BF16)], axis=1)
@@ -169,7 +173,7 @@
     onehot = ones_where(iota((key_rows, entries), 0).astype(F32) == key_row).astype(BF16)
     key = jnp.transpose(jnp.broadcast_to(key_row, (LANES, entries)))
     group = jnp.transpose(jnp.broadcast_to(group_row, (LANES, entries)))
-    here = pl.ds(pl.multiple_of(b * entries, entries), entries)
+    here = span(b, entries)
     keys[here, :] = key
     groups[here, :] = group
     blocks = recv[pl.ds(b * BATCH, BATCH)].reshape(entries, WIDTH)
@@ -183,7 +187,7 @@
 
 def pick(b, picked, keys, groups, fold, spaced, back):
     entries = BATCH * CAP
-    here = pl.ds(pl.multiple_of(b * entries, entries), entries)
+    here = span(b, entries)
     key, group = keys[here, :], groups[here, :]
     lane = iota((entries, LANES), 1).astype(F32)
     onehot = jnp.concatenate(
@@ -296,12 +300,9 @@
                 start()
         return carry
 
-    def fill(n, carry):
+    for n in range(devices // STEP):
         tile = tile_of(n * STEP + iota((1, STEP * CAP), 1) // CAP, gx, gy).astype(F32)
         pack(n, tile, asked, blocks, marks, chunks, codes, picks)
-        return carry
-
-    lax.fori_loop(0, devices // STEP, fill, 0)
     pl.semaphore_wait(barrier, devices - 1)
     lax.fori_loop(0, batches, push, 0)
     for copy in inputs[5:]:
@@ -372,22 +373,14 @@
                 picked[low : low + count, i * LANES : (i + 1) * LANES] = block.astype(BF16)
     keep = pltpu.make_async_copy(back.at[0], returned.at[0], return_sem)
 
-    def give(b, carry):
-        pick(b, picked, keys, groups, fold, spaced, back)
+    for b in range(batches):
+        pick(b, picked, keys, groups, fold, spaced.at[b % 2], back)
         for j, place in enumerate(places(b, gx, gy, False)):
             slot = b * BATCH + j
-
-            def start():
+            if slot == 0:
+                keep.start()
+            else:
                 remote(back.at[slot], returned.at[slot], send_sems.at[2], return_sem, place).start()
-
-            if j == 0:
-                pl.when(b > 0)(start)
-                pl.when(b == 0)(keep.start)
-            else:
-                start()
-        return carry
-
-    lax.fori_loop(0, batches, give, 0)
     for half in range(2):
         for n in range(devices * CAP // 512):
             part = picks[n * 512 : (n + 1) * 512, half * pairs : (half + 1) * pairs].astype(F32)
@@ -468,7 +461,7 @@
             pltpu.VMEM((functions // LANES, functions, LANES), F32),
             pltpu.VMEM((functions, functions), BF16),
             pltpu.VMEM((-(-key_rows // LANES) * LANES, spaced), BF16),
-            pltpu.VMEM((BATCH * CAP, spaced), BF16),
+            pltpu.VMEM((2, BATCH * CAP, spaced), BF16),
             pltpu.VMEM((rows, LANES), F32),
             pltpu.VMEM((4, rows, LANES), F32),
             DMA((3,)),

time: 65.5 us -> 66.6 us (1.017)
  Pallas kernels: 64.7 us -> 65.9 us
    pallas_call x1, Pallas kernels: 63 us -> 64.2 us  [shards(): pl.pallas_call(whole_kernel, name='whole', out_shape=[jax.ShapeDtypeStruc...]
where the time goes in v6:
time: 66.6 us; the launch traced here: 66.5 us
  Pallas kernels  65.9 us (99%)
    pallas_call x1, Pallas kernels, shards(): pl.pallas_call(whole_kernel, name='whole', out_shape=[jax.ShapeDtypeStruc...  64.2 us
    pallas_call x1, Pallas kernels, shards(): pl.pallas_call(finish_kernel, name='finish', out_shape=[jax.ShapeDtypeStr...  1.68 us

profile of v6, /device:TPU:1, one launch (start us, length us, event | category | flops | bytes accessed | tf_op | source)
XLA Modules:
  0.0 66.5 jit_solution(17192556640155286955)
XLA Ops:
  0.6 64.2 %whole.1 = (f32[256,256]{1,0:T(8,128)}, f32[32,64]{1,0:T(8,128)}) custom-call(s32[4,256]{1,0:T(4,128)} %bitcast.7, s32[4,2,256]{2,1,0:T(2,128)} %bitcast.6, s32[2,256]{1,0:T(2,128)} %bitcast.8, bf16[256,256]{1,0:T(8,128)(2,1)} %density_hbm.1, s32[2,72]{1,0:T(2,128)} %bitcast.9, bf16[1152,2048]{1,0:T(8,128)(2,1)} %bitcast.5, ...), custom_call_target="tpu_custom_call" | custom-call | tf_op jit(solution)/shard_map/whole/pallas_call | solution.py:424
  64.8 1.7 %finish.1 = (f32[256,256]{1,0:T(8,128)}, f32[32,64]{1,0:T(8,128)}) custom-call(f32[256,256]{1,0:T(8,128)} %get-tuple-element.4.summed, f32[32,64]{1,0:T(8,128)} %get-tuple-element.5.field), custom_call_target="tpu_custom_call" | custom-call | tf_op jit(solution)/shard_map/finish/pallas_call | solution.py:479

commit v7 on v5

--- a/solution.py
+++ b/solution.py
@@ -222,8 +222,8 @@
     tiles_hbm, slots_hbm, sizes_hbm, density_hbm, extent_hbm, basis_hbm, ones_hbm, spread_hbm, fold_hbm,
     out_hbm, potential_hbm,
     tiles_ref, slots_ref, sizes_ref, density_ref, extent_ref, ones_ref, spread_ref, fold_ref, out_ref, potential_ref,
-    basis, weighted, upright, chunks, recv, back, returned, codes, got, marks, picks, picks_turned, spread, fold, gathered, keys, groups,
-    square, matrix, picked, spaced, charge, halo,
+    basis, permuted, weighted, upright, chunks, recv, back, returned, codes, got, marks, picks, picks_turned, spread, fold, gathered, keys, groups,
+    matrix, picked, spaced, charge, halo,
     send_sems, recv_sems, code_sems, return_sem, halo_send, halo_recv, local_sem,
 ):
     devices = chunks.shape[0]
@@ -261,11 +261,9 @@
     for c in range(column_tiles):
         low, high = (c + 1) * LANES, (c // 3 + 1) * 3 * LANES
         if low < high:
-            square[c, low:high, :] = jnp.zeros((high - low, LANES), F32)
-        low, high = key_offset(c) + GROUPS * (c + 1), key_offset(c + 1)
-        high = picked.shape[0] if c + 1 == column_tiles else high
-        if low < high:
-            picked[low:high, :] = jnp.zeros((high - low, picked.shape[1]), BF16)
+            matrix[low:high, c * LANES : (c + 1) * LANES] = jnp.zeros((high - low, LANES), BF16)
+    low, high = key_offset(column_tiles), picked.shape[0]
+    picked[low:high, :] = jnp.zeros((high - low, picked.shape[1]), BF16)
     for copy in inputs[:5]:
         copy.wait()
     pairs = density_ref.shape[0]
@@ -310,9 +308,12 @@
     fold[...] = fold_ref[...].astype(BF16)
     load.wait()
     mask_basis(basis, extent_ref[...])
+    row, lane = iota((LANES, LANES), 0), iota((LANES, LANES), 1)
+    regroup = ones_where(lane == row % GROUPS * NB + row // GROUPS).astype(BF16)
     for c in range(column_tiles):
         lanes = slice(c * LANES, (c + 1) * LANES)
         upright[:, lanes] = jnp.transpose(basis[lanes, :].astype(F32)).astype(BF16)
+        permuted[lanes, :] = dot(regroup, basis[lanes, :]).astype(BF16)
 
     def arrive(b, carry):
         slots = pl.ds(b * BATCH, BATCH)
@@ -323,12 +324,11 @@
 
     lax.fori_loop(0, batches, arrive, 0)
     for c in range(column_tiles):
-        low = key_offset(c)
-        count = GROUPS * (c + 1)
-        for i in range(NB):
-            block = gathered[low : low + count, i * LANES : (i + 1) * LANES]
-            square[c, pl.ds(i, count, stride=NB), :] = block
-        matrix[:, c * LANES : (c + 1) * LANES] = square[c].astype(BF16)
+        for n in range(c + 1):
+            low = key_offset(c) + n * GROUPS
+            block = [gathered[low : low + GROUPS, i * LANES : (i + 1) * LANES] for i in range(NB)]
+            block = jnp.concatenate(block, axis=0).astype(BF16)
+            matrix[n * LANES : (n + 1) * LANES, c * LANES : (c + 1) * LANES] = block
     step = 2 * LANES
     part = 3 * LANES
     for c in range(cells // step):
@@ -336,7 +336,7 @@
         total = jnp.zeros((1, step), F32)
         for low in range(0, functions, part):
             product = dot(matrix[low : low + part, low:], columns[low:])
-            product = product * columns[low : low + part].astype(F32)
+            product = product * permuted[low : low + part, c * step : (c + 1) * step].astype(F32)
             total = total + jnp.sum(product, axis=0, keepdims=True)
         charge[2 * c : 2 * c + 1, :] = total[:, :LANES]
         charge[2 * c + 1 : 2 * c + 2, :] = total[:, LANES:]
@@ -358,18 +358,23 @@
     potential_out.start()
     for c in range(cells // LANES):
         lanes = slice(c * LANES, (c + 1) * LANES)
-        weighted[:, lanes] = (basis[:, lanes].astype(F32) * potential[c : c + 1]).astype(BF16)
+        weighted[:, lanes] = (permuted[:, lanes].astype(F32) * potential[c : c + 1]).astype(BF16)
     for start in range(0, column_tiles, 2):
         stop = min(start + 2, column_tiles)
         high = stop * LANES
         product = dot(weighted[:high, :], upright[:, start * LANES : high])
         for c in range(start, stop):
-            square[c, :high, :] = product[:, (c - start) * LANES : (c - start + 1) * LANES]
-            low = key_offset(c)
-            count = GROUPS * (c + 1)
-            for i in range(NB):
-                block = square[c, pl.ds(i, count, stride=NB), :]
-                picked[low : low + count, i * LANES : (i + 1) * LANES] = block.astype(BF16)
+            tile = product[:, c * LANES - start * LANES : (c + 1 - start) * LANES]
+            for n in range(0, c + 1, 2):
+                low = key_offset(c) + n * GROUPS
+                for i in range(NB):
+                    pieces = [
+                        tile[m * LANES + i * GROUPS : m * LANES + (i + 1) * GROUPS]
+                        if m <= c else jnp.zeros((GROUPS, LANES), F32)
+                        for m in (n, n + 1)
+                    ]
+                    piece = jnp.concatenate(pieces, axis=0).astype(BF16)
+                    picked[low : low + 2 * GROUPS, i * LANES : (i + 1) * LANES] = piece
     keep = pltpu.make_async_copy(back.at[0], returned.at[0], return_sem)
 
     def give(b, carry):
@@ -450,6 +455,7 @@
             pltpu.VMEM((CX, CY), F32),
             pltpu.VMEM((functions, cells), BF16),
             pltpu.VMEM((functions, cells), BF16),
+            pltpu.VMEM((functions, cells), BF16),
             pltpu.VMEM((cells, functions), BF16),
             chunk,
             chunk,
@@ -465,7 +471,6 @@
             pltpu.VMEM((key_rows, spaced), F32),
             pltpu.VMEM((entries, LANES), F32),
             pltpu.VMEM((entries, LANES), F32),
-            pltpu.VMEM((functions // LANES, functions, LANES), F32),
             pltpu.VMEM((functions, functions), BF16),
             pltpu.VMEM((-(-key_rows // LANES) * LANES, spaced), BF16),
             pltpu.VMEM((BATCH * CAP, spaced), BF16),

time: 65.5 us -> 64.2 us (0.980)
  Pallas kernels: 64.7 us -> 63.4 us
    pallas_call x1, Pallas kernels: 63 us -> 61.8 us  [shards(): pl.pallas_call(whole_kernel, name='whole', out_shape=[jax.ShapeDtypeStruc...]
where the time goes in v7:
time: 64.2 us; the launch traced here: 64.1 us
  Pallas kernels  63.4 us (99%)
    pallas_call x1, Pallas kernels, shards(): pl.pallas_call(whole_kernel, name='whole', out_shape=[jax.ShapeDtypeStruc...  61.8 us
    pallas_call x1, Pallas kernels, shards(): pl.pallas_call(finish_kernel, name='finish', out_shape=[jax.ShapeDtypeStr...  1.68 us

profile of v7, /device:TPU:1, one launch (start us, length us, event | category | flops | bytes accessed | tf_op | source)
XLA Modules:
  0.0 64.1 jit_solution(14538349518959270442)
XLA Ops:
  0.6 61.8 %whole.1 = (f32[256,256]{1,0:T(8,128)}, f32[32,64]{1,0:T(8,128)}) custom-call(s32[4,256]{1,0:T(4,128)} %bitcast.7, s32[4,2,256]{2,1,0:T(2,128)} %bitcast.6, s32[2,256]{1,0:T(2,128)} %bitcast.8, bf16[256,256]{1,0:T(8,128)(2,1)} %density_hbm.1, s32[2,72]{1,0:T(2,128)} %bitcast.9, bf16[1152,2048]{1,0:T(8,128)(2,1)} %bitcast.5, ...), custom_call_target="tpu_custom_call" | custom-call | tf_op jit(solution)/shard_map/whole/pallas_call | solution.py:436
  62.4 1.7 %finish.1 = (f32[256,256]{1,0:T(8,128)}, f32[32,64]{1,0:T(8,128)}) custom-call(f32[256,256]{1,0:T(8,128)} %get-tuple-element.4.summed, f32[32,64]{1,0:T(8,128)} %get-tuple-element.5.field), custom_call_target="tpu_custom_call" | custom-call | tf_op jit(solution)/shard_map/finish/pallas_call | solution.py:491

commit v8 on v7

--- a/solution.py
+++ b/solution.py
@@ -359,8 +359,8 @@
     for c in range(cells // LANES):
         lanes = slice(c * LANES, (c + 1) * LANES)
         weighted[:, lanes] = (permuted[:, lanes].astype(F32) * potential[c : c + 1]).astype(BF16)
-    for start in range(0, column_tiles, 2):
-        stop = min(start + 2, column_tiles)
+    cuts = [0] + list(range(1, column_tiles + 1, 2))
+    for start, stop in zip(cuts, cuts[1:]):
         high = stop * LANES
         product = dot(weighted[:high, :], upright[:, start * LANES : high])
         for c in range(start, stop):

time: 64.2 us -> 63.5 us (0.989)
    pallas_call x1, Pallas kernels: 61.8 us -> 61.1 us  [shards(): pl.pallas_call(whole_kernel, name='whole', out_shape=[jax.ShapeDtypeStruc...]
where the time goes in v8:
time: 63.5 us; the launch traced here: 63.4 us
  Pallas kernels  62.8 us (99%)
  between operations  0.64 us (1%)
    pallas_call x1, Pallas kernels, shards(): pl.pallas_call(whole_kernel, name='whole', out_shape=[jax.ShapeDtypeStruc...  61.1 us
    pallas_call x1, Pallas kernels, shards(): pl.pallas_call(finish_kernel, name='finish', out_shape=[jax.ShapeDtypeStr...  1.68 us

profile of v8, /device:TPU:1, one launch (start us, length us, event | category | flops | bytes accessed | tf_op | source)
XLA Modules:
  0.0 63.4 jit_solution(17452096811604686398)
XLA Ops:
  0.6 61.1 %whole.1 = (f32[256,256]{1,0:T(8,128)}, f32[32,64]{1,0:T(8,128)}) custom-call(s32[4,256]{1,0:T(4,128)} %bitcast.7, s32[4,2,256]{2,1,0:T(2,128)} %bitcast.6, s32[2,256]{1,0:T(2,128)} %bitcast.8, bf16[256,256]{1,0:T(8,128)(2,1)} %density_hbm.1, s32[2,72]{1,0:T(2,128)} %bitcast.9, bf16[1152,2048]{1,0:T(8,128)(2,1)} %bitcast.5, ...), custom_call_target="tpu_custom_call" | custom-call | tf_op jit(solution)/shard_map/whole/pallas_call | solution.py:436
  61.7 1.7 %finish.1 = (f32[256,256]{1,0:T(8,128)}, f32[32,64]{1,0:T(8,128)}) custom-call(f32[256,256]{1,0:T(8,128)} %get-tuple-element.4.summed, f32[32,64]{1,0:T(8,128)} %get-tuple-element.5.field), custom_call_target="tpu_custom_call" | custom-call | tf_op jit(solution)/shard_map/finish/pallas_call | solution.py:491

commit v9 on v8

--- a/solution.py
+++ b/solution.py
@@ -259,8 +259,8 @@
     lax.fori_loop(0, batches, greet, 0)
     gathered[...] = jnp.zeros_like(gathered)
     for c in range(column_tiles):
-        low, high = (c + 1) * LANES, (c // 3 + 1) * 3 * LANES
-        if low < high:
+        low, high = (c + 1) * LANES, (c + 2) * LANES
+        if c % 2 == 1:
             matrix[low:high, c * LANES : (c + 1) * LANES] = jnp.zeros((high - low, LANES), BF16)
     low, high = key_offset(column_tiles), picked.shape[0]
     picked[low:high, :] = jnp.zeros((high - low, picked.shape[1]), BF16)
@@ -330,13 +330,13 @@
             block = jnp.concatenate(block, axis=0).astype(BF16)
             matrix[n * LANES : (n + 1) * LANES, c * LANES : (c + 1) * LANES] = block
     step = 2 * LANES
-    part = 3 * LANES
+    parts = [0] + list(range(LANES, functions + 1, 2 * LANES))
     for c in range(cells // step):
         columns = basis[:, c * step : (c + 1) * step]
         total = jnp.zeros((1, step), F32)
-        for low in range(0, functions, part):
-            product = dot(matrix[low : low + part, low:], columns[low:])
-            product = product * permuted[low : low + part, c * step : (c + 1) * step].astype(F32)
+        for low, high in zip(parts, parts[1:]):
+            product = dot(matrix[low:high, low:], columns[low:])
+            product = product * permuted[low:high, c * step : (c + 1) * step].astype(F32)
             total = total + jnp.sum(product, axis=0, keepdims=True)
         charge[2 * c : 2 * c + 1, :] = total[:, :LANES]
         charge[2 * c + 1 : 2 * c + 2, :] = total[:, LANES:]

time: 63.5 us -> 62.9 us (level)
  Pallas kernels: 62.8 us -> 62.1 us
    pallas_call x1, Pallas kernels: 61.1 us -> 60.4 us  [shards(): pl.pallas_call(whole_kernel, name='whole', out_shape=[jax.ShapeDtypeStruc...]
where the time goes in v9:
time: 62.9 us; the launch traced here: 62.7 us
  Pallas kernels  62.1 us (99%)
  between operations  0.64 us (1%)
    pallas_call x1, Pallas kernels, shards(): pl.pallas_call(whole_kernel, name='whole', out_shape=[jax.ShapeDtypeStruc...  60.4 us
    pallas_call x1, Pallas kernels, shards(): pl.pallas_call(finish_kernel, name='finish', out_shape=[jax.ShapeDtypeStr...  1.68 us

profile of v9, /device:TPU:1, one launch (start us, length us, event | category | flops | bytes accessed | tf_op | source)
XLA Modules:
  0.0 62.7 jit_solution(8504205169887442332)
XLA Ops:
  0.6 60.4 %whole.1 = (f32[256,256]{1,0:T(8,128)}, f32[32,64]{1,0:T(8,128)}) custom-call(s32[4,256]{1,0:T(4,128)} %bitcast.7, s32[4,2,256]{2,1,0:T(2,128)} %bitcast.6, s32[2,256]{1,0:T(2,128)} %bitcast.8, bf16[256,256]{1,0:T(8,128)(2,1)} %density_hbm.1, s32[2,72]{1,0:T(2,128)} %bitcast.9, bf16[1152,2048]{1,0:T(8,128)(2,1)} %bitcast.5, ...), custom_call_target="tpu_custom_call" | custom-call | tf_op jit(solution)/shard_map/whole/pallas_call | solution.py:436
  61.1 1.7 %finish.1 = (f32[256,256]{1,0:T(8,128)}, f32[32,64]{1,0:T(8,128)}) custom-call(f32[256,256]{1,0:T(8,128)} %get-tuple-element.4.summed, f32[32,64]{1,0:T(8,128)} %get-tuple-element.5.field), custom_call_target="tpu_custom_call" | custom-call | tf_op jit(solution)/shard_map/finish/pallas_call | solution.py:491
